TPU v7x, 32 devices: a whole 2x2x4 slice. The times are simulated.
32 devices in a mesh: dp: 4 (over y, core), tensor: 8 (over z, x).
Axes of the slice: x: 2, y: 2, z: 4, core: 2. Of those that a mesh axis runs over, the one named last changes fastest.
Arguments:
- thinker_rows: bfloat16 [8192, 8192], P('dp', 'tensor'), may hold values from -6 to 6
- proj_weight: bfloat16 [8192, 3584], P('tensor'), may hold values from -0.0625 to 0.0625
- proj_bias: float32 [3584], replicated, may hold values from -3 to 3
- cotangent: bfloat16 [8192, 3584], P('dp'), may hold values from -6 to 6
- block_owner: int32 [64], P('dp'), may hold values from 0 to 3, as said below
- block_offset: int32 [64], P('dp'), may hold values from 0 to 31, as said below
Outputs:
- grad_thinker: bfloat16 [16384, 8192], P('dp', 'tensor')
- proj_grad: float32 [8192, 3584], P(('tensor', 'dp'))
Inputs may be any that keep to these rules, and one draw needn't show every extreme that they name: `block_owner`: the 16 blocks of one index of dp name at most 8 blocks for any one owner, and the blocks for one owner stand next to each other; one owner receives exactly 8 blocks from every index of dp. `block_offset`: no two talker blocks share both owner and offset.
All inputs are finite; a program needn't handle non-finite values.
Results may differ from a plain program's by a relative error of at most 0.015.
Values may be sent and summed in bfloat16 or wider, within the bound.
No kernel may reach another device: no remote copies, remote signals or barrier semaphores. Data moves between devices by JAX's collectives and lax.ppermute only.
A program may use at most 128 MiB of HBM per device.

v0:
```python
import jax
import jax.numpy as jnp
from jax import lax
from jax.sharding import PartitionSpec as P

BLOCK = 128


def slope_of(summed, proj_bias, cot_rows):
    pre_act = summed + proj_bias
    gate_value = jax.nn.sigmoid(pre_act)
    return (
        cot_rows.astype(jnp.float32) * gate_value * (1.0 + pre_act * (1.0 - gate_value))
    ).astype(jnp.bfloat16)


def return_rows(input_grad, block_owner, block_offset, dp_count):
    row_count, local_width = input_grad.shape
    block_total = row_count // BLOCK
    slot_cap = 2 * block_total // dp_count
    slot_total = dp_count * slot_cap
    pieces = input_grad.reshape(block_total, BLOCK, local_width)
    owner_hot = (block_owner[:, None] == jnp.arange(dp_count, dtype=jnp.int32)[None, :]).astype(
        jnp.int32
    )
    within = jnp.sum((jnp.cumsum(owner_hot, axis=0) - owner_hot) * owner_hot, axis=1)
    slot_index = block_owner * slot_cap + within
    slot_match = slot_index[None, :] == jnp.arange(slot_total, dtype=jnp.int32)[:, None]
    filled = jnp.any(slot_match, axis=1)
    picked = jnp.sum(
        jnp.where(slot_match, jnp.arange(block_total, dtype=jnp.int32)[None, :], 0), axis=1
    )
    send_rows = jnp.where(filled[:, None, None], pieces[picked], jnp.zeros((), jnp.bfloat16))
    send_rows = send_rows.reshape(dp_count, slot_cap, BLOCK, local_width)
    send_offset = jnp.where(filled, block_offset[picked], -1).reshape(dp_count, slot_cap)
    got_rows, got_offset = (
        lax.all_to_all(send_rows, "dp", split_axis=0, concat_axis=0, tiled=True),
        lax.all_to_all(send_offset, "dp", split_axis=0, concat_axis=0, tiled=True),
    )
    chooser = (
        got_offset.reshape(slot_total)[None, :]
        == jnp.arange(2 * block_total, dtype=jnp.int32)[:, None]
    ).astype(jnp.bfloat16)
    owner_grad = jnp.dot(
        chooser,
        got_rows.reshape(slot_total, BLOCK * local_width),
        preferred_element_type=jnp.float32,
    )
    return owner_grad.astype(jnp.bfloat16).reshape(2 * block_total * BLOCK, local_width)


def shards(thinker_rows, proj_weight, proj_bias, cotangent, block_owner, block_offset):
    row_count, local_width = thinker_rows.shape
    tensor_count = lax.axis_size("tensor")
    dp_count = lax.axis_size("dp")
    share_rows = row_count // tensor_count
    summed = lax.psum_scatter(
        jnp.dot(thinker_rows, proj_weight, preferred_element_type=jnp.float32).astype(jnp.bfloat16),
        "tensor",
        scatter_dimension=0,
        tiled=True,
    ).astype(jnp.float32)
    own_cot = lax.dynamic_slice_in_dim(
        cotangent, lax.axis_index("tensor") * share_rows, share_rows, 0
    )
    slope_rows = lax.all_gather(slope_of(summed, proj_bias, own_cot), "tensor", axis=0, tiled=True)
    input_grad = lax.dot_general(
        slope_rows, proj_weight, (((1,), (1,)), ((), ())), preferred_element_type=jnp.float32
    ).astype(jnp.bfloat16)
    grad_scale = float(row_count * dp_count) ** (-0.5)
    weight_term = (
        lax.dot_general(
            thinker_rows, slope_rows, (((0,), (0,)), ((), ())), preferred_element_type=jnp.float32
        )
        * grad_scale
    )
    proj_grad = lax.psum_scatter(
        weight_term.astype(jnp.bfloat16), "dp", scatter_dimension=0, tiled=True
    ).astype(jnp.float32)
    grad_thinker = return_rows(input_grad, block_owner, block_offset, dp_count)
    return (grad_thinker, proj_grad)


def solution(mesh):
    return jax.shard_map(
        shards,
        mesh=mesh,
        in_specs=(P("dp", "tensor"), P("tensor", None), P(), P("dp", None), P("dp"), P("dp")),
        out_specs=(P("dp", "tensor"), P(("tensor", "dp"), None)),
        check_vma=False,
    )
```

profile of v0, /device:TPU:0, one launch (start us, length us, event | category | flops | bytes accessed | tf_op | source)
XLA Modules:
  0.0 688.4 jit_solution(17571851615024074190)
XLA Ops:
  7.2 0.0 copy-start
  7.2 0.0 reduce-scatter.3.cloned.1.call-start
  7.2 21.9 %convolution_convert_fusion.1 = bf16[2048,3584]{1,0:T(8,128)(2,1)} fusion(bf16[2048,1024]{1,0:T(8,128)(2,1)} %param.6, bf16[1024,3584]{1,0:T(8,128)(2,1)} %param.7), kind=kOutput, calls=%fused_computation.3 | convolution fusion | flops 15039725568 | bytes 26214400 | tf_op jit(solution)/shard_map/dot_general | solution.py:58
  29.2 0.0 copy-start.2
  29.2 0.0 reduce-scatter.3.cloned.1.call-update
  29.2 0.0 all-gather.2.cloned.1.call-start
  29.2 239.3 %reduce-scatter.3.cloned.1.call-done = bf16[256,3584]{1,0:T(8,128)(2,1)} async-done(((bf16[2048,3584]{1,0:T(8,128)(2,1)}), bf16[256,3584]{1,0:T(8,128)(2,1)}) %reduce-scatter.3.cloned.1.call-update) | async-done | bytes 1835024 | tf_op jit(solution)/shard_map/reduce_scatter | solution.py:57
  268.6 0.0 copy-done.2
  268.6 4.8 multiply_convert_fusion.1
  273.4 0.0 all-gather.2.cloned.1.call-update
  273.4 0.2 reduce-scatter.5.cloned.1.call-start
  273.6 201.0 %all-gather.2.cloned.1.call-done = bf16[2048,3584]{1,0:T(8,128)(2,1)} async-done(((bf16[256,3584]{1,0:T(8,128)(2,1)}), bf16[2048,3584]{1,0:T(8,128)(2,1)}) %all-gather.2.cloned.1.call-update) | async-done | bytes 14680080 | tf_op jit(solution)/shard_map/all_gather | solution.py:66
  474.7 21.8 %fusion = bf16[1024,3584]{0,1:T(8,128)(2,1)} fusion(bf16[2048,3584]{1,0:T(8,128)(2,1)} %all-gather.2.cloned.1.call-done, bf16[2048,1024]{1,0:T(8,128)(2,1)} %param.6), kind=kOutput, calls=%fused_computation.6 | convolution fusion | flops 15039725568 | bytes 26214400 | tf_op jit(solution)/shard_map/dot_general | solution.py:72
  496.5 0.0 copy-start.3
  496.5 0.0 reduce-scatter.5.cloned.1.call-update
  496.5 0.6 copy-done.3
  497.1 0.1 fusion.3
  497.2 0.2 select_reduce_fusion.1
  497.4 0.1 select_reduce_fusion
  497.5 0.0 copy-done
  497.6 0.7 gather_fusion
  498.3 0.1 fusion.2
  498.4 0.7 select_n.41
  499.0 3.2 all-to-all-start
  502.3 0.1 broadcast_in_dim.43
  502.3 23.2 %convolution_convert_fusion.2 = bf16[2048,1024]{1,0:T(8,128)(2,1)} fusion(bf16[2048,3584]{1,0:T(8,128)(2,1)} %all-gather.2.cloned.1.call-done, bf16[1024,3584]{1,0:T(8,128)(2,1)} %param.7), kind=kOutput, calls=%fused_computation.7 | convolution fusion | flops 15034482688 | bytes 26214400 | tf_op jit(solution)/shard_map/dot_general | solution.py:67
  525.5 7.3 %gather_fusion.1 = bf16[32,128,1024]{2,1,0:T(8,128)(2,1)} fusion(bf16[16,128,1024]{2,1,0:T(8,128)(2,1)} %bitcast.21, s32[1024]{0:T(1024)S(1)} %pad_clamp_fusion), kind=kCustom, calls=%fused_computation.1 | custom fusion | bytes 16777344 | tf_op jit(solution)/shard_map/gather | solution.py:33
  532.8 7.4 %broadcast_select_fusion = bf16[4,8,128,1024]{3,2,1,0:T(8,128)(2,1)} fusion(bf16[4,8,128,1024]{3,2,1,0:T(8,128)(2,1)} %bitcast.20, pred[4,8]{1,0:T(4,128)(4,1)S(1)} %broadcast_in_dim.43), kind=kLoop, calls=%fused_computation.5 | loop fusion | flops 4194304 | bytes 16777248 | tf_op jit(solution)/shard_map/jit(_where)/select_n | solution.py:33
  540.2 0.0 all-to-all-done
  540.2 5.9 all-to-all-start.1
  546.1 0.5 broadcast.65
  546.6 0.7 reduce.3
  547.3 0.1 eq.47
  547.4 101.1 %all-to-all-done.1 = bf16[4,8,128,1024]{3,2,1,0:T(8,128)(2,1)} async-done(((bf16[4,8,128,1024]{3,2,1,0:T(8,128)(2,1)}), bf16[4,8,128,1024]{3,2,1,0:T(8,128)(2,1)}, u32[]{:S(2)}, u32[]{:S(2)}) %all-to-all-start.1) | async-done | bytes 8388640 | tf_op jit(solution)/shard_map/all_to_all | solution.py:37
  648.5 11.6 %copy.14 = bf16[4,8,128,1024]{3,1,2,0:T(8,128)(2,1)} copy(bf16[4,8,128,1024]{3,2,1,0:T(8,128)(2,1)} %all-to-all-done.1) | data formatting | bytes 16777216
  660.1 0.0 copy-start.1
  660.1 8.9 %convolution_convert_fusion = bf16[32,131072]{1,0:T(8,128)(2,1)} fusion(bf16[32,131072]{1,0:T(8,128)(2,1)} %bitcast.19, s32[32]{0:T(128)S(1)} %eq.47), kind=kOutput, calls=%fused_computation.2 | convolution fusion | flops 272630784 | bytes 16777344 | tf_op jit(solution)/shard_map/dot_general | solution.py:44
  669.0 8.9 %reshape.62 = bf16[4096,1024]{1,0:T(8,128)(2,1)} reshape(bf16[32,131072]{1,0:T(8,128)(2,1)} %convolution_convert_fusion) | data formatting | bytes 16777216 | tf_op jit(solution)/shard_map/reshape | solution.py:49
  677.9 0.0 reduce-scatter.5.cloned.1.call-done
  677.9 4.0 copy.13
  681.9 0.0 copy-done.1
  (5 shorter events, 0.1 us)
Async XLA Ops:
  7.2 490.4 %copy-start = (s32[16]{0:T(128)S(1)}, s32[16]{0:T(128)}, u32[]{:S(2)}) copy-start(s32[16]{0:T(128)} %param.11) | copy-start | bytes 196
  7.2 261.4 %reduce-scatter.3.cloned.1.call-start = ((), (), s32[]{:S(2)}) async-start(), calls=%async_computation.4 | async-start | bytes 16515072 | tf_op jit(solution)/shard_map/reduce_scatter | solution.py:57
  29.2 239.4 %copy-start.2 = (f32[3584]{0:T(1024)S(1)}, f32[3584]{0:T(1024)}, u32[]{:S(2)}) copy-start(f32[3584]{0:T(1024)} %param.8) | copy-start | bytes 43012
  29.2 445.5 %all-gather.2.cloned.1.call-start = ((), (), s32[]{:S(2)}) async-start(), calls=%async_computation.5 | async-start | bytes 16515072 | tf_op jit(solution)/shard_map/all_gather | solution.py:66
  273.4 404.5 %reduce-scatter.5.cloned.1.call-start = ((), (), s32[]{:S(2)}) async-start(), calls=%async_computation.6 | async-start | bytes 9175040 | tf_op jit(solution)/shard_map/reduce_scatter | solution.py:77
  496.5 0.7 copy-start.3
  499.0 41.2 %all-to-all-start = ((s32[4,1,8]{2,1,0:T(1,128)}), s32[4,1,8]{2,1,0:T(1,128)S(1)}, u32[]{:S(2)}, u32[]{:S(2)}) async-start(s32[4,1,8]{2,1,0:T(1,128)} %bitcast.2), calls=%async_computation | async-start | bytes 4096 | tf_op jit(solution)/shard_map/all_to_all | solution.py:38
  540.2 108.3 %all-to-all-start.1 = ((bf16[4,8,128,1024]{3,2,1,0:T(8,128)(2,1)}), bf16[4,8,128,1024]{3,2,1,0:T(8,128)(2,1)}, u32[]{:S(2)}, u32[]{:S(2)}) async-start(bf16[4,8,128,1024]{3,2,1,0:T(8,128)(2,1)} %broadcast_select_fusion), calls=%async_computation.2 | async-start | bytes 16777216 | tf_op jit(solution)/shard_map/all_to_all | solution.py:37
  660.1 21.8 %copy-start.1 = (s32[16]{0:T(128)S(1)}, s32[16]{0:T(128)}, u32[]{:S(2)}) copy-start(s32[16]{0:T(128)} %param.11) | copy-start | bytes 196
Sparse Core Ops, SparseCore 0:
  29.3 239.2 reduce-scatter.2
  273.5 201.1 all-gather.1
  496.6 72.9 reduce-scatter.4
where the time goes:
time: 689 us; the launch traced here: 688 us
  waiting for transfers between devices  542 us (79%)
  matrix products  75.9 us (11%)
  local copies, waits for them, and re-layouts  34.4 us (5%)
  between operations  13.8 us (2%)
  other arithmetic  13.3 us (2%)
  starting transfers between devices  9.4 us (1%)
    reduce_scatter x1, waiting for transfers between devices, shards(): lax.psum_scatter(jnp.dot(thinker_rows, proj_weight, preferred_element_typ...  239 us
    all_gather x1, waiting for transfers between devices, shards(): lax.all_gather(slope_of(summed, proj_bias, own_cot), 'tensor', axis=0, ti...  201 us
    all_to_all x1, waiting for transfers between devices, return_rows(): lax.all_to_all(send_rows, 'dp', split_axis=0, concat_axis=0, tiled=True)  101 us
    dot_general x1, matrix products, shards(): lax.dot_general(slope_rows, proj_weight, (((1,), (1,)), ((), ())), prefer...  23.2 us
    dot_general x1, matrix products, shards(): jnp.dot(thinker_rows, proj_weight, preferred_element_type=jnp.float32)  21.9 us
    dot_general x1, matrix products, shards(): lax.dot_general(thinker_rows, slope_rows, (((0,), (0,)), ((), ())), prefe...  21.8 us
    unnamed x10, local copies, waits for them, and re-layouts  16.2 us
  transfers between devices with their start and end apart: 5, of which 3 were waited for; matrix products, arithmetic and copies ran while one was open for 10% of the time, Pallas kernels for 0%

commit v1 on v0

v1 whole, which is shorter than its diff:
```python
import jax
import jax.numpy as jnp
from jax import lax
from jax.experimental import pallas as pl
from jax.experimental.pallas import tpu as pltpu
from jax.sharding import PartitionSpec as P

BLOCK = 128
LANES = 256
F32 = jnp.float32
BF16 = jnp.bfloat16


def split_units(total, unit, parts):
    units = total // unit
    parts = min(parts, units)
    sizes = [units // parts] * parts
    middle = sorted(range(parts), key=lambda i: abs(2 * i - parts + 1))
    for i in middle[: units % parts]:
        sizes[i] += 1
    spans, start = [], 0
    for size in sizes:
        spans.append((start * unit, size * unit))
        start += size
    return spans


class Grid:
    def __init__(self, tensor_count, dp_count):
        self.nx = 1 << ((tensor_count.bit_length() - 1) // 2)
        self.nz = tensor_count // self.nx
        self.nc = 2
        self.ny = dp_count // self.nc
        t, d = lax.axis_index("tensor"), lax.axis_index("dp")
        self.z, self.x = t // self.nx, t % self.nx
        self.y, self.c = d // self.nc, d % self.nc
        self.d = d

    def swap_x(self, value, k):
        pairs = [(z * self.nx + x, z * self.nx + (x ^ k)) for z in range(self.nz) for x in range(self.nx)]
        return lax.ppermute(value, "tensor", pairs)

    def hop_z(self, value, h):
        moves = [(h, h + 1), (self.nz - 1 - h, self.nz - 2 - h)]
        pairs = [(a * self.nx + x, b * self.nx + x) for a, b in moves for x in range(self.nx)]
        return lax.ppermute(value, "tensor", pairs)

    def swap_y(self, value, k):
        pairs = [(y * self.nc + c, (y ^ k) * self.nc + c) for y in range(self.ny) for c in range(self.nc)]
        return lax.ppermute(value, "dp", pairs)

    def swap_core(self, value):
        return lax.ppermute(value, "dp", [(d, d ^ 1) for d in range(self.ny * self.nc)])


def rows_at(value, start, count):
    return lax.dynamic_slice_in_dim(value, start, count, 0)


def product(a, b, dims):
    return lax.dot_general(a, b, (dims, ((), ())), preferred_element_type=F32)


def place_blocks(pieces, piece_owner, piece_offset, taken, me, out_blocks, width):
    per = pieces[0].shape[0]
    count = len(pieces)

    def kernel(owner_ref, offset_ref, taken_ref, me_ref, *refs):
        sources, out_ref, zero_ref, sems, zero_sems = refs[:count], *refs[count:]
        zero_ref[...] = jnp.zeros_like(zero_ref)
        mine = me_ref[0]

        def copy(i, j):
            n = i * per + j
            return pltpu.make_async_copy(sources[i].at[j], out_ref.at[offset_ref[n]], sems.at[n])

        def clear(n):
            return pltpu.make_async_copy(zero_ref, out_ref.at[n], zero_sems.at[n])

        for i in range(count):
            for j in range(per):
                pl.when(owner_ref[i * per + j] == mine)(lambda: copy(i, j).start())
        for n in range(out_blocks):
            pl.when(taken_ref[n] == 0)(lambda: clear(n).start())
        for i in range(count):
            for j in range(per):
                pl.when(owner_ref[i * per + j] == mine)(lambda: copy(i, j).wait())
        for n in range(out_blocks):
            pl.when(taken_ref[n] == 0)(lambda: clear(n).wait())

    smem = pl.BlockSpec(memory_space=pltpu.SMEM)
    hbm = pl.BlockSpec(memory_space=pl.ANY)
    return pl.pallas_call(
        kernel,
        out_shape=jax.ShapeDtypeStruct((out_blocks, BLOCK, width), BF16),
        in_specs=[smem] * 4 + [hbm] * count,
        out_specs=hbm,
        scratch_shapes=[
            pltpu.VMEM((BLOCK, width), BF16),
            pltpu.SemaphoreType.DMA((count * per,)),
            pltpu.SemaphoreType.DMA((out_blocks,)),
        ],
        name="place_blocks",
    )(piece_owner, piece_offset, taken, me, *pieces)


def shards(thinker_rows, proj_weight, proj_bias, cotangent, block_owner, block_offset):
    g = Grid(lax.axis_size("tensor"), lax.axis_size("dp"))
    row_count, width = thinker_rows.shape
    dp_count = g.ny * g.nc
    out_width = proj_weight.shape[1]
    x_rows = row_count // g.nx
    x_blocks = x_rows // BLOCK
    nr = min(4, x_blocks)
    r_rows = x_rows // nr
    r_blocks = r_rows // BLOCK
    spans = split_units(out_width, LANES, 4)
    ne = len(spans)
    share = width // dp_count
    xs = range(1, g.nx)

    tables = lax.all_gather(jnp.stack([block_owner, block_offset]), "dp", axis=0)

    def weight_from_x(e):
        start, size = spans[e]
        mine = lax.dynamic_slice(proj_weight, (g.d * share, start), (share, size))
        whole = {}
        for k in xs:
            got = g.swap_x(mine, k)
            parts = {0: got}
            for ky in range(1, g.ny):
                parts[ky * g.nc] = g.swap_y(got, ky)
            for key in list(parts):
                parts[key ^ 1] = g.swap_core(parts[key])
            full = jnp.zeros((width, size), BF16)
            for key, part in parts.items():
                full = lax.dynamic_update_slice(full, part, ((g.d ^ key) * share, 0))
            whole[k] = full
        return whole

    def rows_from_x(r):
        return {k: g.swap_x(rows_at(thinker_rows, (g.x ^ k) * x_rows + r * r_rows, r_rows), k) for k in xs}

    own_rows = [rows_at(thinker_rows, g.x * x_rows + r * r_rows, r_rows) for r in range(nr)]
    own_weight = [proj_weight[:, start : start + size] for start, size in spans]
    x_weight = [None] * ne
    x_rows_got = [None] * nr
    x_weight[0] = weight_from_x(0)
    for r in range(nr):
        x_rows_got[r] = rows_from_x(r)
    for e in range(1, ne):
        x_weight[e] = weight_from_x(e)

    def slope_piece(r, e):
        start, size = spans[e]
        part = product(own_rows[r], own_weight[e], ((1,), (0,)))
        for k in xs:
            part = part + product(x_rows_got[r][k], x_weight[e][k], ((1,), (0,)))
        part = part.astype(BF16)
        total = part.astype(F32)
        send = part
        for h in range(g.nz - 1):
            got = g.hop_z(send, h).astype(F32)
            total = total + got
            send = (part.astype(F32) + got).astype(BF16)
        pre_act = total + proj_bias[start : start + size]
        gate = jax.nn.sigmoid(pre_act)
        cot = lax.dynamic_slice(cotangent, (g.x * x_rows + r * r_rows, start), (r_rows, size))
        return (cot.astype(F32) * gate * (1.0 + pre_act * (1.0 - gate))).astype(BF16)

    def weight_grad(e, pieces):
        slope = jnp.concatenate(pieces, axis=0)
        size = slope.shape[1]
        terms = {}
        for k in range(g.nx):
            left = jnp.concatenate([own_rows[r] if k == 0 else x_rows_got[r][k] for r in range(nr)], axis=0)
            term = product(left, slope, ((0,), (0,))).astype(BF16)
            term = term.reshape(g.ny, g.nc, share, size)
            keep = lax.dynamic_index_in_dim(term, g.c, 1, keepdims=False)
            give = lax.dynamic_index_in_dim(term, 1 - g.c, 1, keepdims=False)
            terms[k] = keep.astype(F32) + g.swap_core(give).astype(F32)
        total = terms[0]
        for k in xs:
            total = total + g.swap_x(terms[k].astype(BF16), k).astype(F32)
        mine = lax.dynamic_index_in_dim(total, g.y, 0, keepdims=False)
        for ky in range(1, g.ny):
            give = lax.dynamic_index_in_dim(total, g.y ^ ky, 0, keepdims=False).astype(BF16)
            mine = mine + g.swap_y(give, ky).astype(F32)
        return mine * float(row_count * dp_count) ** (-0.5)

    placed, placed_at = [], []

    def return_rows(r, pieces):
        slope = jnp.concatenate(pieces, axis=1)
        found = {}
        for k in range(g.nx):
            weight = proj_weight if k == 0 else jnp.concatenate([x_weight[e][k] for e in range(ne)], axis=1)
            grad = product(slope, weight, ((1,), (1,))).astype(BF16)
            found[(k, 0, 0)] = grad if k == 0 else g.swap_x(grad, k)
        for k in range(g.nx):
            for ky in range(1, g.ny):
                found[(k, ky, 0)] = g.swap_y(found[(k, 0, 0)], ky)
            for ky in range(g.ny):
                found[(k, ky, 1)] = g.swap_core(found[(k, ky, 0)])
        for (k, ky, kc), piece in found.items():
            placed.append(piece.reshape(r_blocks, BLOCK, width))
            placed_at.append((g.d ^ (ky * g.nc + kc), (g.x ^ k) * x_blocks + r * r_blocks))

    slopes = {}
    early = ne // 2
    order = [(r, e) for e in range(early) for r in range(nr)]
    order += [(r, e) for r in range(nr) for e in range(early, ne)]
    grads = [None] * ne
    for r, e in order:
        slopes[r, e] = slope_piece(r, e)
        if r == nr - 1:
            grads[e] = weight_grad(e, [slopes[i, e] for i in range(nr)])
        if e == ne - 1:
            return_rows(r, [slopes[r, i] for i in range(ne)])

    sources = jnp.stack([lax.dynamic_slice(tables, (d, 0, at), (1, 2, r_blocks))[0] for d, at in placed_at])
    piece_owner = sources[:, 0].reshape(-1)
    piece_offset = sources[:, 1].reshape(-1)
    out_blocks = 2 * row_count // BLOCK
    taken = jnp.any(
        (piece_owner == g.d)[None, :] & (piece_offset[None, :] == jnp.arange(out_blocks)[:, None]), axis=1
    ).astype(jnp.int32)
    grad_thinker = place_blocks(placed, piece_owner, piece_offset, taken, g.d[None], out_blocks, width)
    return grad_thinker.reshape(out_blocks * BLOCK, width), jnp.concatenate(grads, axis=1)


def solution(mesh):
    return jax.shard_map(
        shards,
        mesh=mesh,
        in_specs=(P("dp", "tensor"), P("tensor", None), P(), P("dp", None), P("dp"), P("dp")),
        out_specs=(P("dp", "tensor"), P(("tensor", "dp"), None)),
        check_vma=False,
    )
```

time: 689 us -> 919 us (1.33)
  the two profiles are of different devices: /device:TPU:0 before, /device:TPU:21 now
where the time goes in v1:
time: 919 us; the launch traced here: 908 us
  waiting for transfers between devices  284 us (31%)
  Pallas kernels  257 us (28%)
  starting transfers between devices  197 us (21%)
  matrix products  94.5 us (10%)
  other arithmetic  39.6 us (4%)
  local copies, waits for them, and re-layouts  28 us (3%)
    pallas_call x1, Pallas kernels, place_blocks(): pl.pallas_call(kernel, out_shape=jax.ShapeDtypeStruct((out_blocks, BLOCK,...  257 us
    ppermute x48, waiting for transfers between devices, hop_z(): return lax.ppermute(value, 'tensor', pairs)  179 us
    dot_general x48, matrix products, product(): return lax.dot_general(a, b, (dims, ((), ())), preferred_element_type=F32)  94.5 us
    ppermute x48, starting transfers between devices, hop_z(): return lax.ppermute(value, 'tensor', pairs)  90.6 us
    ppermute x32, starting transfers between devices, swap_core(): lax.ppermute(value, 'dp', [(d, d ^ 1) for d in range(self.ny * self.nc)])  83.9 us
    ppermute x16, waiting for transfers between devices, swap_x(): return lax.ppermute(value, 'tensor', pairs)  79.1 us
    ppermute x16, waiting for transfers between devices, swap_y(): return lax.ppermute(value, 'dp', pairs)  25.3 us
    convert_element_type x6, other arithmetic, slope_piece(): (cot.astype(F32) * gate * (1.0 + pre_act * (1.0 - gate))).astype(BF16)  18.5 us
  transfers between devices with their start and end apart: 112, of which 45 were waited for; matrix products, arithmetic and copies ran while one was open for 16% of the time, Pallas kernels for 28%

profile of v1, /device:TPU:21, one launch (start us, length us, event | category | flops | bytes accessed | tf_op | source)
XLA Modules:
  0.0 908.0 jit_solution(634983001185528156)
XLA Ops:
  40.6 16.6 %collective-permute-done.22 = bf16[256,768]{1,0:T(8,128)(2,1)} collective-permute-done((bf16[256,768]{1,0:T(8,128)(2,1)}, bf16[256,768]{1,0:T(8,128)(2,1)}, u32[]{:S(2)}, u32[]{:S(2)}) %collective-permute-start.22) | collective-permute-done | bytes 393248 | tf_op jit(solution)/shard_map/ppermute | solution.py:41
  68.6 11.0 %collective-permute-done.8 = bf16[256,1024]{1,0:T(8,128)(2,1)S(1)} collective-permute-done((bf16[256,1024]{1,0:T(8,128)(2,1)S(1)}, bf16[256,1024]{1,0:T(8,128)(2,1)S(1)}, u32[]{:S(2)}, u32[]{:S(2)}) %collective-permute-start.8) | collective-permute-done | bytes 524320 | tf_op jit(solution)/shard_map/ppermute | solution.py:41
  82.6 8.2 collective-permute-done.15
  95.6 7.0 collective-permute-done.9
  107.3 6.6 collective-permute-done.16
  141.1 5.2 collective-permute-done.77
  147.8 7.0 collective-permute-done.26
  156.2 7.0 collective-permute-done.5
  164.6 7.0 collective-permute-done.46
  173.1 7.0 collective-permute-done.66
  182.3 6.2 collective-permute-done.86
  194.0 4.7 collective-permute-done.58
  200.9 6.2 collective-permute-done.78
  209.3 6.2 collective-permute-done.27
  217.8 6.2 collective-permute-done.6
  226.2 6.2 collective-permute-done.47
  234.6 6.2 collective-permute-done.67
  242.2 7.0 collective-permute-done.87
  259.5 5.6 collective-permute-done.12
  266.9 9.5 %collective-permute-done.43 = bf16[256,1024]{1,0:T(8,128)(2,1)S(1)} collective-permute-done((bf16[256,1024]{1,0:T(8,128)(2,1)S(1)}, bf16[256,1024]{1,0:T(8,128)(2,1)S(1)}, u32[]{:S(2)}, u32[]{:S(2)}) %collective-permute-start.43) | collective-permute-done | bytes 524320 | tf_op jit(solution)/shard_map/ppermute | solution.py:46
  277.9 9.7 %collective-permute-done.63 = bf16[256,1024]{1,0:T(8,128)(2,1)S(1)} collective-permute-done((bf16[256,1024]{1,0:T(8,128)(2,1)S(1)}, bf16[256,1024]{1,0:T(8,128)(2,1)S(1)}, u32[]{:S(2)}, u32[]{:S(2)}) %collective-permute-start.63) | collective-permute-done | bytes 524320 | tf_op jit(solution)/shard_map/ppermute | solution.py:46
  289.1 9.7 %collective-permute-done.83 = bf16[256,1024]{1,0:T(8,128)(2,1)S(1)} collective-permute-done((bf16[256,1024]{1,0:T(8,128)(2,1)S(1)}, bf16[256,1024]{1,0:T(8,128)(2,1)S(1)}, u32[]{:S(2)}, u32[]{:S(2)}) %collective-permute-start.83) | collective-permute-done | bytes 524320 | tf_op jit(solution)/shard_map/ppermute | solution.py:46
  325.4 6.4 collective-permute-done.88
  352.0 9.8 %collective-permute-start.96 = (bf16[2,256,768]{2,1,0:T(8,128)(2,1)S(1)}, bf16[2,256,768]{2,1,0:T(8,128)(2,1)S(1)}, u32[]{:S(2)}, u32[]{:S(2)}) collective-permute-start(bf16[2,256,768]{2,1,0:T(8,128)(2,1)S(1)} %dynamic-slice_bitcast_fusion.7), channel_id=1, source_target_pairs={{0,8},{8,0},{16,24},{24,16},{1,9},{9,1},{17,25},{25,17},{2,10},{10... | collective-permute-start | bytes 2359304 | tf_op jit(solution)/shard_map/ppermute | solution.py:53
  364.7 9.7 %collective-permute-done.44 = bf16[256,1024]{1,0:T(8,128)(2,1)S(1)} collective-permute-done((bf16[256,1024]{1,0:T(8,128)(2,1)S(1)}, bf16[256,1024]{1,0:T(8,128)(2,1)S(1)}, u32[]{:S(2)}, u32[]{:S(2)}) %collective-permute-start.44) | collective-permute-done | bytes 524320 | tf_op jit(solution)/shard_map/ppermute | solution.py:46
  376.0 9.7 %collective-permute-done.64 = bf16[256,1024]{1,0:T(8,128)(2,1)S(1)} collective-permute-done((bf16[256,1024]{1,0:T(8,128)(2,1)S(1)}, bf16[256,1024]{1,0:T(8,128)(2,1)S(1)}, u32[]{:S(2)}, u32[]{:S(2)}) %collective-permute-start.64) | collective-permute-done | bytes 524320 | tf_op jit(solution)/shard_map/ppermute | solution.py:46
  387.2 9.7 %collective-permute-done.84 = bf16[256,1024]{1,0:T(8,128)(2,1)S(1)} collective-permute-done((bf16[256,1024]{1,0:T(8,128)(2,1)S(1)}, bf16[256,1024]{1,0:T(8,128)(2,1)S(1)}, u32[]{:S(2)}, u32[]{:S(2)}) %collective-permute-start.84) | collective-permute-done | bytes 524320 | tf_op jit(solution)/shard_map/ppermute | solution.py:46
  396.9 5.1 collective-permute-start.97
  415.8 10.5 %collective-permute-done.65 = bf16[256,1024]{1,0:T(8,128)(2,1)S(1)} collective-permute-done((bf16[256,1024]{1,0:T(8,128)(2,1)S(1)}, bf16[256,1024]{1,0:T(8,128)(2,1)S(1)}, u32[]{:S(2)}, u32[]{:S(2)}) %collective-permute-start.65) | collective-permute-done | bytes 524320 | tf_op jit(solution)/shard_map/ppermute | solution.py:46
  426.3 4.9 collective-permute-start.21
  431.2 6.3 collective-permute-done.85
  437.5 5.1 collective-permute-start.14
  450.8 5.4 convolution_convert_fusion.9
  460.6 6.2 convolution_convert_fusion.11
  471.2 6.2 convolution_convert_fusion.13
  483.5 5.3 convolution_convert_fusion.15
  499.0 7.2 collective-permute-done.89
  511.1 7.7 collective-permute-done.69
  522.6 7.5 collective-permute-done.49
  541.7 5.0 collective-permute-start.101
  552.8 5.7 collective-permute-done.98
  559.4 5.0 collective-permute-start.105
  564.4 4.9 all-gather.1
  589.5 7.2 collective-permute-start.72
  599.3 6.2 collective-permute-start.54
  613.3 6.2 collective-permute-start.32
  626.9 7.7 collective-permute-start.95
  645.6 256.8 %place_blocks.1 = bf16[32,128,1024]{2,1,0:T(8,128)(2,1)} custom-call(s32[64]{0:T(128)} %copy-done.117, s32[64]{0:T(128)} %copy-done.118, s32[32]{0:T(128)} %convert_element_type.647.taken_ref, s32[1]{0:T(128)} %bitcast.3.me_ref, bf16[2,128,1024]{2,1,0:T(8,128)(2,1)} %bitcast.204, bf16[2,128,1024]{2,1,0:T(8,128)(2,1)} %bitcast.216, ...), custom_call_target="tpu_custom_call" | custom-call | tf_op jit(solution)/shard_map/place_blocks/pallas_call | solution.py:93
  (609 shorter events, 310.4 us)
Async XLA Ops:
  4.7 55.2 %collective-permute-start.36 = (bf16[256,1024]{1,0:T(8,128)(2,1)}, bf16[256,1024]{1,0:T(8,128)(2,1)S(1)}, u32[]{:S(2)}, u32[]{:S(2)}) collective-permute-start(bf16[256,1024]{1,0:T(8,128)(2,1)} %get-tuple-element.25), channel_id=1, source_target_pairs={{0,1},{1,0},{2,3},{3,2},{4,5},{5,4},{6,7},{7,6},{8,9},{9,8},{10,11... | collective-permute-start | bytes 1572872 | tf_op jit(solution)/shard_map/ppermute | solution.py:41
  8.2 30.9 %collective-permute-start.1 = (bf16[256,768]{1,0:T(8,128)(2,1)}, bf16[256,768]{1,0:T(8,128)(2,1)}, u32[]{:S(2)}, u32[]{:S(2)}) collective-permute-start(bf16[256,768]{1,0:T(8,128)(2,1)} %get-tuple-element.18), channel_id=1, source_target_pairs={{0,1},{1,0},{2,3},{3,2},{4,5},{5,4},{6,7},{7,6},{8,9},{9,8},{10,11... | collective-permute-start | bytes 1179656 | tf_op jit(solution)/shard_map/ppermute | solution.py:41
  8.4 51.8 %collective-permute-start.56 = (bf16[256,1024]{1,0:T(8,128)(2,1)}, bf16[256,1024]{1,0:T(8,128)(2,1)S(1)}, u32[]{:S(2)}, u32[]{:S(2)}) collective-permute-start(bf16[256,1024]{1,0:T(8,128)(2,1)} %get-tuple-element.23), channel_id=1, source_target_pairs={{0,1},{1,0},{2,3},{3,2},{4,5},{5,4},{6,7},{7,6},{8,9},{9,8},{10,11... | collective-permute-start | bytes 1572872 | tf_op jit(solution)/shard_map/ppermute | solution.py:41
  9.6 49.9 %collective-permute-start = (bf16[256,1024]{1,0:T(8,128)(2,1)}, bf16[256,1024]{1,0:T(8,128)(2,1)S(1)}, u32[]{:S(2)}, u32[]{:S(2)}) collective-permute-start(bf16[256,1024]{1,0:T(8,128)(2,1)} %get-tuple-element.27), channel_id=1, source_target_pairs={{0,1},{1,0},{2,3},{3,2},{4,5},{5,4},{6,7},{7,6},{8,9},{9,8},{10,11... | collective-permute-start | bytes 1572872 | tf_op jit(solution)/shard_map/ppermute | solution.py:41
  9.9 47.3 %collective-permute-start.22 = (bf16[256,768]{1,0:T(8,128)(2,1)}, bf16[256,768]{1,0:T(8,128)(2,1)}, u32[]{:S(2)}, u32[]{:S(2)}) collective-permute-start(bf16[256,768]{1,0:T(8,128)(2,1)} %get-tuple-element.19), channel_id=1, source_target_pairs={{0,1},{1,0},{2,3},{3,2},{4,5},{5,4},{6,7},{7,6},{8,9},{9,8},{10,11... | collective-permute-start | bytes 1179656 | tf_op jit(solution)/shard_map/ppermute | solution.py:41
  39.1 29.2 %collective-permute-start.76 = (bf16[256,1024]{1,0:T(8,128)(2,1)}, bf16[256,1024]{1,0:T(8,128)(2,1)S(1)}, u32[]{:S(2)}, u32[]{:S(2)}) collective-permute-start(bf16[256,1024]{1,0:T(8,128)(2,1)} %get-tuple-element.22), channel_id=1, source_target_pairs={{0,1},{1,0},{2,3},{3,2},{4,5},{5,4},{6,7},{7,6},{8,9},{9,8},{10,11... | collective-permute-start | bytes 1572872 | tf_op jit(solution)/shard_map/ppermute | solution.py:41
  59.6 31.2 %collective-permute-start.15 = (bf16[256,1024]{1,0:T(8,128)(2,1)S(1)}, bf16[256,1024]{1,0:T(8,128)(2,1)S(1)}, u32[]{:S(2)}, u32[]{:S(2)}) collective-permute-start(bf16[256,1024]{1,0:T(8,128)(2,1)S(1)} %copy-done.53), channel_id=1, source_target_pairs={{0,1},{1,0},{2,3},{3,2},{4,5},{5,4},{6,7},{7,6},{8,9},{9,8},{10,11... | collective-permute-start | bytes 1572872 | tf_op jit(solution)/shard_map/ppermute | solution.py:41
  59.9 31.4 %collective-permute-start.2 = (bf16[256,768]{1,0:T(8,128)(2,1)}, bf16[256,768]{1,0:T(8,128)(2,1)S(1)}, u32[]{:S(2)}, u32[]{:S(2)}) collective-permute-start(bf16[256,768]{1,0:T(8,128)(2,1)} %collective-permute-done.1), channel_id=1, source_target_pairs={{0,16},{8,24},{16,0},{24,8},{1,17},{9,25},{17,1},{25,9},{2,18},{10... | collective-permute-start | bytes 1179656 | tf_op jit(solution)/shard_map/ppermute | solution.py:50
  60.3 34.6 %collective-permute-start.3 = (bf16[256,768]{1,0:T(8,128)(2,1)}, bf16[256,768]{1,0:T(8,128)(2,1)S(1)}, u32[]{:S(2)}, u32[]{:S(2)}) collective-permute-start(bf16[256,768]{1,0:T(8,128)(2,1)} %collective-permute-done.1), channel_id=1, source_target_pairs={{0,8},{8,0},{16,24},{24,16},{1,9},{9,1},{17,25},{25,17},{2,10},{10... | collective-permute-start | bytes 1179656 | tf_op jit(solution)/shard_map/ppermute | solution.py:53
  127.2 27.6 %collective-permute-start.26 = (bf16[256,768]{1,0:T(8,128)(2,1)S(1)}, bf16[256,768]{1,0:T(8,128)(2,1)S(1)}, u32[]{:S(2)}, u32[]{:S(2)}) collective-permute-start(bf16[256,768]{1,0:T(8,128)(2,1)S(1)} %fusion.33), channel_id=1, source_target_pairs={{0,2},{1,3},{6,4},{7,5},{8,10},{9,11},{14,12},{15,13},{16,18},{17,... | collective-permute-start | bytes 1179656 | tf_op jit(solution)/shard_map/ppermute | solution.py:46
  133.0 30.2 %collective-permute-start.5 = (bf16[256,768]{1,0:T(8,128)(2,1)S(1)}, bf16[256,768]{1,0:T(8,128)(2,1)S(1)}, u32[]{:S(2)}, u32[]{:S(2)}) collective-permute-start(bf16[256,768]{1,0:T(8,128)(2,1)S(1)} %fusion.32), channel_id=1, source_target_pairs={{0,2},{1,3},{6,4},{7,5},{8,10},{9,11},{14,12},{15,13},{16,18},{17,... | collective-permute-start | bytes 1179656 | tf_op jit(solution)/shard_map/ppermute | solution.py:46
  138.3 33.3 %collective-permute-start.46 = (bf16[256,768]{1,0:T(8,128)(2,1)S(1)}, bf16[256,768]{1,0:T(8,128)(2,1)S(1)}, u32[]{:S(2)}, u32[]{:S(2)}) collective-permute-start(bf16[256,768]{1,0:T(8,128)(2,1)S(1)} %fusion.35), channel_id=1, source_target_pairs={{0,2},{1,3},{6,4},{7,5},{8,10},{9,11},{14,12},{15,13},{16,18},{17,... | collective-permute-start | bytes 1179656 | tf_op jit(solution)/shard_map/ppermute | solution.py:46
  139.7 40.4 %collective-permute-start.66 = (bf16[256,768]{1,0:T(8,128)(2,1)S(1)}, bf16[256,768]{1,0:T(8,128)(2,1)S(1)}, u32[]{:S(2)}, u32[]{:S(2)}) collective-permute-start(bf16[256,768]{1,0:T(8,128)(2,1)S(1)} %fusion.37), channel_id=1, source_target_pairs={{0,2},{1,3},{6,4},{7,5},{8,10},{9,11},{14,12},{15,13},{16,18},{17,... | collective-permute-start | bytes 1179656 | tf_op jit(solution)/shard_map/ppermute | solution.py:46
  146.4 42.1 %collective-permute-start.86 = (bf16[256,768]{1,0:T(8,128)(2,1)S(1)}, bf16[256,768]{1,0:T(8,128)(2,1)S(1)}, u32[]{:S(2)}, u32[]{:S(2)}) collective-permute-start(bf16[256,768]{1,0:T(8,128)(2,1)S(1)} %fusion.39), channel_id=1, source_target_pairs={{0,2},{1,3},{6,4},{7,5},{8,10},{9,11},{14,12},{15,13},{16,18},{17,... | collective-permute-start | bytes 1179656 | tf_op jit(solution)/shard_map/ppermute | solution.py:46
  154.8 95.9 %collective-permute-start.40 = (bf16[256,1024]{1,0:T(8,128)(2,1)S(1)}, bf16[256,1024]{1,0:T(8,128)(2,1)S(1)}, u32[]{:S(2)}, u32[]{:S(2)}) collective-permute-start(bf16[256,1024]{1,0:T(8,128)(2,1)S(1)} %fusion.26), channel_id=1, source_target_pairs={{0,2},{1,3},{6,4},{7,5},{8,10},{9,11},{14,12},{15,13},{16,18},{17,... | collective-permute-start | bytes 1572872 | tf_op jit(solution)/shard_map/ppermute | solution.py:46
  163.2 89.0 %collective-permute-start.60 = (bf16[256,1024]{1,0:T(8,128)(2,1)S(1)}, bf16[256,1024]{1,0:T(8,128)(2,1)S(1)}, u32[]{:S(2)}, u32[]{:S(2)}) collective-permute-start(bf16[256,1024]{1,0:T(8,128)(2,1)S(1)} %fusion.28), channel_id=1, source_target_pairs={{0,2},{1,3},{6,4},{7,5},{8,10},{9,11},{14,12},{15,13},{16,18},{17,... | collective-permute-start | bytes 1572872 | tf_op jit(solution)/shard_map/ppermute | solution.py:46
  171.7 82.0 %collective-permute-start.80 = (bf16[256,1024]{1,0:T(8,128)(2,1)S(1)}, bf16[256,1024]{1,0:T(8,128)(2,1)S(1)}, u32[]{:S(2)}, u32[]{:S(2)}) collective-permute-start(bf16[256,1024]{1,0:T(8,128)(2,1)S(1)} %fusion.30), channel_id=1, source_target_pairs={{0,2},{1,3},{6,4},{7,5},{8,10},{9,11},{14,12},{15,13},{16,18},{17,... | collective-permute-start | bytes 1572872 | tf_op jit(solution)/shard_map/ppermute | solution.py:46
  252.2 35.4 %collective-permute-start.63 = (bf16[256,1024]{1,0:T(8,128)(2,1)S(1)}, bf16[256,1024]{1,0:T(8,128)(2,1)S(1)}, u32[]{:S(2)}, u32[]{:S(2)}) collective-permute-start(bf16[256,1024]{1,0:T(8,128)(2,1)S(1)} %fusion.29), channel_id=1, source_target_pairs={{0,2},{1,3},{6,4},{7,5},{8,10},{9,11},{14,12},{15,13},{16,18},{17,... | collective-permute-start | bytes 1572872 | tf_op jit(solution)/shard_map/ppermute | solution.py:46
  253.7 45.2 %collective-permute-start.83 = (bf16[256,1024]{1,0:T(8,128)(2,1)S(1)}, bf16[256,1024]{1,0:T(8,128)(2,1)S(1)}, u32[]{:S(2)}, u32[]{:S(2)}) collective-permute-start(bf16[256,1024]{1,0:T(8,128)(2,1)S(1)} %fusion.31), channel_id=1, source_target_pairs={{0,2},{1,3},{6,4},{7,5},{8,10},{9,11},{14,12},{15,13},{16,18},{17,... | collective-permute-start | bytes 1572872 | tf_op jit(solution)/shard_map/ppermute | solution.py:46
  255.2 45.2 %collective-permute-start.39 = (bf16[256,768]{1,0:T(8,128)(2,1)S(1)}, bf16[256,768]{1,0:T(8,128)(2,1)S(1)}, u32[]{:S(2)}, u32[]{:S(2)}) collective-permute-start(bf16[256,768]{1,0:T(8,128)(2,1)S(1)} %fusion.98), channel_id=1, source_target_pairs={{4,6},{5,7},{2,0},{3,1},{12,14},{13,15},{10,8},{11,9},{20,22},{21,... | collective-permute-start | bytes 1179656 | tf_op jit(solution)/shard_map/ppermute | solution.py:46
  265.2 36.6 %collective-permute-start.59 = (bf16[256,768]{1,0:T(8,128)(2,1)S(1)}, bf16[256,768]{1,0:T(8,128)(2,1)S(1)}, u32[]{:S(2)}, u32[]{:S(2)}) collective-permute-start(bf16[256,768]{1,0:T(8,128)(2,1)S(1)} %fusion.104), channel_id=1, source_target_pairs={{4,6},{5,7},{2,0},{3,1},{12,14},{13,15},{10,8},{11,9},{20,22},{21,... | collective-permute-start | bytes 1179656 | tf_op jit(solution)/shard_map/ppermute | solution.py:46
  276.4 26.7 %collective-permute-start.79 = (bf16[256,768]{1,0:T(8,128)(2,1)S(1)}, bf16[256,768]{1,0:T(8,128)(2,1)S(1)}, u32[]{:S(2)}, u32[]{:S(2)}) collective-permute-start(bf16[256,768]{1,0:T(8,128)(2,1)S(1)} %fusion.110), channel_id=1, source_target_pairs={{4,6},{5,7},{2,0},{3,1},{12,14},{13,15},{10,8},{11,9},{20,22},{21,... | collective-permute-start | bytes 1179656 | tf_op jit(solution)/shard_map/ppermute | solution.py:46
  303.1 28.7 %collective-permute-start.88 = (bf16[256,768]{1,0:T(8,128)(2,1)S(1)}, bf16[256,768]{1,0:T(8,128)(2,1)S(1)}, u32[]{:S(2)}, u32[]{:S(2)}) collective-permute-start(bf16[256,768]{1,0:T(8,128)(2,1)S(1)} %fusion.113), channel_id=1, source_target_pairs={{4,6},{5,7},{2,0},{3,1},{12,14},{13,15},{10,8},{11,9},{20,22},{21,... | collective-permute-start | bytes 1179656 | tf_op jit(solution)/shard_map/ppermute | solution.py:46
  307.1 34.1 %collective-permute-start.41 = (bf16[256,1024]{1,0:T(8,128)(2,1)S(1)}, bf16[256,1024]{1,0:T(8,128)(2,1)S(1)}, u32[]{:S(2)}, u32[]{:S(2)}) collective-permute-start(bf16[256,1024]{1,0:T(8,128)(2,1)S(1)} %fusion.84), channel_id=1, source_target_pairs={{2,4},{3,5},{4,2},{5,3},{10,12},{11,13},{12,10},{13,11},{18,20},{1... | collective-permute-start | bytes 1572872 | tf_op jit(solution)/shard_map/ppermute | solution.py:46
  309.2 35.5 %collective-permute-start.61 = (bf16[256,1024]{1,0:T(8,128)(2,1)S(1)}, bf16[256,1024]{1,0:T(8,128)(2,1)S(1)}, u32[]{:S(2)}, u32[]{:S(2)}) collective-permute-start(bf16[256,1024]{1,0:T(8,128)(2,1)S(1)} %fusion.86), channel_id=1, source_target_pairs={{2,4},{3,5},{4,2},{5,3},{10,12},{11,13},{12,10},{13,11},{18,20},{1... | collective-permute-start | bytes 1572872 | tf_op jit(solution)/shard_map/ppermute | solution.py:46
  318.7 28.3 %collective-permute-start.81 = (bf16[256,1024]{1,0:T(8,128)(2,1)S(1)}, bf16[256,1024]{1,0:T(8,128)(2,1)S(1)}, u32[]{:S(2)}, u32[]{:S(2)}) collective-permute-start(bf16[256,1024]{1,0:T(8,128)(2,1)S(1)} %fusion.88), channel_id=1, source_target_pairs={{2,4},{3,5},{4,2},{5,3},{10,12},{11,13},{12,10},{13,11},{18,20},{1... | collective-permute-start | bytes 1572872 | tf_op jit(solution)/shard_map/ppermute | solution.py:46
  323.3 28.6 %collective-permute-start.20 = (bf16[256,1024]{1,0:T(8,128)(2,1)S(1)}, bf16[256,1024]{1,0:T(8,128)(2,1)S(1)}, u32[]{:S(2)}, u32[]{:S(2)}) collective-permute-start(bf16[256,1024]{1,0:T(8,128)(2,1)S(1)} %fusion.83), channel_id=1, source_target_pairs={{2,4},{3,5},{4,2},{5,3},{10,12},{11,13},{12,10},{13,11},{18,20},{1... | collective-permute-start | bytes 1572872 | tf_op jit(solution)/shard_map/ppermute | solution.py:46
  331.8 31.4 %collective-permute-start.13 = (bf16[256,1024]{1,0:T(8,128)(2,1)S(1)}, bf16[256,1024]{1,0:T(8,128)(2,1)S(1)}, u32[]{:S(2)}, u32[]{:S(2)}) collective-permute-start(bf16[256,1024]{1,0:T(8,128)(2,1)S(1)} %fusion.82), channel_id=1, source_target_pairs={{2,4},{3,5},{4,2},{5,3},{10,12},{11,13},{12,10},{13,11},{18,20},{1... | collective-permute-start | bytes 1572872 | tf_op jit(solution)/shard_map/ppermute | solution.py:46
  341.2 33.2 %collective-permute-start.44 = (bf16[256,1024]{1,0:T(8,128)(2,1)S(1)}, bf16[256,1024]{1,0:T(8,128)(2,1)S(1)}, u32[]{:S(2)}, u32[]{:S(2)}) collective-permute-start(bf16[256,1024]{1,0:T(8,128)(2,1)S(1)} %fusion.85), channel_id=1, source_target_pairs={{2,4},{3,5},{4,2},{5,3},{10,12},{11,13},{12,10},{13,11},{18,20},{1... | collective-permute-start | bytes 1572872 | tf_op jit(solution)/shard_map/ppermute | solution.py:46
  344.7 41.0 %collective-permute-start.64 = (bf16[256,1024]{1,0:T(8,128)(2,1)S(1)}, bf16[256,1024]{1,0:T(8,128)(2,1)S(1)}, u32[]{:S(2)}, u32[]{:S(2)}) collective-permute-start(bf16[256,1024]{1,0:T(8,128)(2,1)S(1)} %fusion.87), channel_id=1, source_target_pairs={{2,4},{3,5},{4,2},{5,3},{10,12},{11,13},{12,10},{13,11},{18,20},{1... | collective-permute-start | bytes 1572872 | tf_op jit(solution)/shard_map/ppermute | solution.py:46
  347.0 50.0 %collective-permute-start.84 = (bf16[256,1024]{1,0:T(8,128)(2,1)S(1)}, bf16[256,1024]{1,0:T(8,128)(2,1)S(1)}, u32[]{:S(2)}, u32[]{:S(2)}) collective-permute-start(bf16[256,1024]{1,0:T(8,128)(2,1)S(1)} %fusion.89), channel_id=1, source_target_pairs={{2,4},{3,5},{4,2},{5,3},{10,12},{11,13},{12,10},{13,11},{18,20},{1... | collective-permute-start | bytes 1572872 | tf_op jit(solution)/shard_map/ppermute | solution.py:46
  352.0 142.0 %collective-permute-start.96 = (bf16[2,256,768]{2,1,0:T(8,128)(2,1)S(1)}, bf16[2,256,768]{2,1,0:T(8,128)(2,1)S(1)}, u32[]{:S(2)}, u32[]{:S(2)}) collective-permute-start(bf16[2,256,768]{2,1,0:T(8,128)(2,1)S(1)} %dynamic-slice_bitcast_fusion.7), channel_id=1, source_target_pairs={{0,8},{8,0},{16,24},{24,16},{1,9},{9,1},{17,25},{25,17},{2,10},{10... | collective-permute-start | bytes 2359304 | tf_op jit(solution)/shard_map/ppermute | solution.py:53
  363.2 39.0 %collective-permute-start.42 = (bf16[256,1024]{1,0:T(8,128)(2,1)S(1)}, bf16[256,1024]{1,0:T(8,128)(2,1)S(1)}, u32[]{:S(2)}, u32[]{:S(2)}) collective-permute-start(bf16[256,1024]{1,0:T(8,128)(2,1)S(1)} %fusion.48), channel_id=1, source_target_pairs={{4,6},{5,7},{2,0},{3,1},{12,14},{13,15},{10,8},{11,9},{20,22},{21,... | collective-permute-start | bytes 1572872 | tf_op jit(solution)/shard_map/ppermute | solution.py:46
  374.5 29.1 %collective-permute-start.62 = (bf16[256,1024]{1,0:T(8,128)(2,1)S(1)}, bf16[256,1024]{1,0:T(8,128)(2,1)S(1)}, u32[]{:S(2)}, u32[]{:S(2)}) collective-permute-start(bf16[256,1024]{1,0:T(8,128)(2,1)S(1)} %fusion.54), channel_id=1, source_target_pairs={{4,6},{5,7},{2,0},{3,1},{12,14},{13,15},{10,8},{11,9},{20,22},{21,... | collective-permute-start | bytes 1572872 | tf_op jit(solution)/shard_map/ppermute | solution.py:46
  396.9 99.8 %collective-permute-start.97 = (bf16[2,256,768]{2,1,0:T(8,128)(2,1)S(1)}, bf16[2,256,768]{2,1,0:T(8,128)(2,1)S(1)}, u32[]{:S(2)}, u32[]{:S(2)}) collective-permute-start(bf16[2,256,768]{2,1,0:T(8,128)(2,1)S(1)} %dynamic-slice_bitcast_fusion.6), channel_id=1, source_target_pairs={{0,8},{8,0},{16,24},{24,16},{1,9},{9,1},{17,25},{25,17},{2,10},{10... | collective-permute-start | bytes 2359304 | tf_op jit(solution)/shard_map/ppermute | solution.py:53
  404.9 32.6 %collective-permute-start.85 = (bf16[256,1024]{1,0:T(8,128)(2,1)S(1)}, bf16[256,1024]{1,0:T(8,128)(2,1)S(1)}, u32[]{:S(2)}, u32[]{:S(2)}) collective-permute-start(bf16[256,1024]{1,0:T(8,128)(2,1)S(1)} %fusion.63), channel_id=1, source_target_pairs={{4,6},{5,7},{2,0},{3,1},{12,14},{13,15},{10,8},{11,9},{20,22},{21,... | collective-permute-start | bytes 1572872 | tf_op jit(solution)/shard_map/ppermute | solution.py:46
  415.0 82.3 %collective-permute-start.108 = (bf16[2,256,768]{2,1,0:T(8,128)(2,1)S(1)}, bf16[2,256,768]{2,1,0:T(8,128)(2,1)S(1)}, u32[]{:S(2)}, u32[]{:S(2)}) collective-permute-start(bf16[2,256,768]{2,1,0:T(8,128)(2,1)S(1)} %dynamic-slice_bitcast_fusion.5), channel_id=1, source_target_pairs={{0,8},{8,0},{16,24},{24,16},{1,9},{9,1},{17,25},{25,17},{2,10},{10... | collective-permute-start | bytes 2359304 | tf_op jit(solution)/shard_map/ppermute | solution.py:53
  426.3 51.1 %collective-permute-start.21 = (bf16[256,1024]{1,0:T(8,128)(2,1)S(1)}, bf16[256,1024]{1,0:T(8,128)(2,1)}, u32[]{:S(2)}, u32[]{:S(2)}) collective-permute-start(bf16[256,1024]{1,0:T(8,128)(2,1)S(1)} %fusion.45), channel_id=1, source_target_pairs={{4,6},{5,7},{2,0},{3,1},{12,14},{13,15},{10,8},{11,9},{20,22},{21,... | collective-permute-start | bytes 1572872 | tf_op jit(solution)/shard_map/ppermute | solution.py:46
  437.5 40.9 %collective-permute-start.14 = (bf16[256,1024]{1,0:T(8,128)(2,1)S(1)}, bf16[256,1024]{1,0:T(8,128)(2,1)}, u32[]{:S(2)}, u32[]{:S(2)}) collective-permute-start(bf16[256,1024]{1,0:T(8,128)(2,1)S(1)} %fusion.42), channel_id=1, source_target_pairs={{4,6},{5,7},{2,0},{3,1},{12,14},{13,15},{10,8},{11,9},{20,22},{21,... | collective-permute-start | bytes 1572872 | tf_op jit(solution)/shard_map/ppermute | solution.py:46
  534.9 41.6 %collective-permute-start.100 = (bf16[2,256,1024]{2,1,0:T(8,128)(2,1)S(1)}, bf16[2,256,1024]{2,1,0:T(8,128)(2,1)}, u32[]{:S(2)}, u32[]{:S(2)}) collective-permute-start(bf16[2,256,1024]{2,1,0:T(8,128)(2,1)S(1)} %dynamic-slice_bitcast_fusion.3), channel_id=1, source_target_pairs={{0,8},{8,0},{16,24},{24,16},{1,9},{9,1},{17,25},{25,17},{2,10},{10... | collective-permute-start | bytes 3145736 | tf_op jit(solution)/shard_map/ppermute | solution.py:53
  541.7 37.7 %collective-permute-start.101 = (bf16[2,256,1024]{2,1,0:T(8,128)(2,1)}, bf16[2,256,1024]{2,1,0:T(8,128)(2,1)}, u32[]{:S(2)}, u32[]{:S(2)}) collective-permute-start(bf16[2,256,1024]{2,1,0:T(8,128)(2,1)} %dynamic-slice_bitcast_fusion.2), channel_id=1, source_target_pairs={{0,8},{8,0},{16,24},{24,16},{1,9},{9,1},{17,25},{25,17},{2,10},{10... | collective-permute-start | bytes 3145736 | tf_op jit(solution)/shard_map/ppermute | solution.py:53
  546.7 32.9 %collective-permute-start.104 = (bf16[2,256,1024]{2,1,0:T(8,128)(2,1)}, bf16[2,256,1024]{2,1,0:T(8,128)(2,1)}, u32[]{:S(2)}, u32[]{:S(2)}) collective-permute-start(bf16[2,256,1024]{2,1,0:T(8,128)(2,1)} %dynamic-slice_bitcast_fusion.1), channel_id=1, source_target_pairs={{0,8},{8,0},{16,24},{24,16},{1,9},{9,1},{17,25},{25,17},{2,10},{10... | collective-permute-start | bytes 3145736 | tf_op jit(solution)/shard_map/ppermute | solution.py:53
  546.7 28.8 %collective-permute-start.110 = (bf16[2,256,768]{2,1,0:T(8,128)(2,1)}, bf16[2,256,768]{2,1,0:T(8,128)(2,1)}, u32[]{:S(2)}, u32[]{:S(2)}) collective-permute-start(bf16[2,256,768]{2,1,0:T(8,128)(2,1)} %fusion.4), channel_id=1, source_target_pairs={{0,1},{1,0},{2,3},{3,2},{4,5},{5,4},{6,7},{7,6},{8,9},{9,8},{10,11... | collective-permute-start | bytes 2359304 | tf_op jit(solution)/shard_map/ppermute | solution.py:41
  586.6 26.7 %collective-permute-start.102 = (bf16[2,256,1024]{2,1,0:T(8,128)(2,1)S(1)}, bf16[2,256,1024]{2,1,0:T(8,128)(2,1)S(1)}, u32[]{:S(2)}, u32[]{:S(2)}) collective-permute-start(bf16[2,256,1024]{2,1,0:T(8,128)(2,1)S(1)} %fusion.2), channel_id=1, source_target_pairs={{0,1},{1,0},{2,3},{3,2},{4,5},{5,4},{6,7},{7,6},{8,9},{9,8},{10,11... | collective-permute-start | bytes 3145736 | tf_op jit(solution)/shard_map/ppermute | solution.py:41
  597.7 29.2 %collective-permute-start.106 = (bf16[2,256,1024]{2,1,0:T(8,128)(2,1)S(1)}, bf16[2,256,1024]{2,1,0:T(8,128)(2,1)S(1)}, u32[]{:S(2)}, u32[]{:S(2)}) collective-permute-start(bf16[2,256,1024]{2,1,0:T(8,128)(2,1)S(1)} %fusion), channel_id=1, source_target_pairs={{0,1},{1,0},{2,3},{3,2},{4,5},{5,4},{6,7},{7,6},{8,9},{9,8},{10,11... | collective-permute-start | bytes 3145736 | tf_op jit(solution)/shard_map/ppermute | solution.py:41
  611.3 26.1 %collective-permute-start.34 = (bf16[256,1024]{1,0:T(8,128)(2,1)S(1)}, bf16[256,1024]{1,0:T(8,128)(2,1)S(1)}, u32[]{:S(2)}, u32[]{:S(2)}) collective-permute-start(bf16[256,1024]{1,0:T(8,128)(2,1)S(1)} %copy-done.52), channel_id=1, source_target_pairs={{0,8},{8,0},{16,24},{24,16},{1,9},{9,1},{17,25},{25,17},{2,10},{10... | collective-permute-start | bytes 1572872 | tf_op jit(solution)/shard_map/ppermute | solution.py:53
  641.0 261.4 %collective-permute-start.103 = (bf16[256,1024]{1,0:T(8,128)(2,1)}, bf16[256,1024]{1,0:T(8,128)(2,1)}, u32[]{:S(2)}, u32[]{:S(2)}) collective-permute-start(bf16[256,1024]{1,0:T(8,128)(2,1)} %fusion.124), channel_id=1, source_target_pairs={{0,16},{8,24},{16,0},{24,8},{1,17},{9,25},{17,1},{25,9},{2,18},{10... | collective-permute-start | bytes 1572872 | tf_op jit(solution)/shard_map/ppermute | solution.py:50
  642.1 261.7 %collective-permute-start.107 = (bf16[256,1024]{1,0:T(8,128)(2,1)}, bf16[256,1024]{1,0:T(8,128)(2,1)}, u32[]{:S(2)}, u32[]{:S(2)}) collective-permute-start(bf16[256,1024]{1,0:T(8,128)(2,1)} %fusion.125), channel_id=1, source_target_pairs={{0,16},{8,24},{16,0},{24,8},{1,17},{9,25},{17,1},{25,9},{2,18},{10... | collective-permute-start | bytes 1572872 | tf_op jit(solution)/shard_map/ppermute | solution.py:50
  (188 other events, 2341.1 us)

commit v2 on v0

v2 whole, which is shorter than its diff:
```python
import jax
import jax.numpy as jnp
from jax import lax
from jax.experimental import pallas as pl
from jax.experimental.pallas import tpu as pltpu
from jax.sharding import PartitionSpec as P

BLOCK = 128
LANES = 256
F32 = jnp.float32
BF16 = jnp.bfloat16
CUTS = (4 / 14, 8 / 14, 11 / 14)
GATHERED = 1
COST = 3.0


class Grid:
    def __init__(self, tensor_count, dp_count):
        self.nx = 1 << ((tensor_count.bit_length() - 1) // 2)
        self.nz = tensor_count // self.nx
        self.nc = 2
        self.ny = dp_count // self.nc
        t, d = lax.axis_index("tensor"), lax.axis_index("dp")
        self.z, self.x = t // self.nx, t % self.nx
        self.y, self.c = d // self.nc, d % self.nc
        self.d = d

    def swap_x(self, value, k):
        pairs = [(z * self.nx + x, z * self.nx + (x ^ k)) for z in range(self.nz) for x in range(self.nx)]
        return lax.ppermute(value, "tensor", pairs)

    def hop_z(self, value, h):
        moves = [(h, h + 1), (self.nz - 1 - h, self.nz - 2 - h)]
        pairs = [(a * self.nx + x, b * self.nx + x) for a, b in moves for x in range(self.nx)]
        return lax.ppermute(value, "tensor", pairs)

    def swap_y(self, value, k):
        pairs = [(y * self.nc + c, (y ^ k) * self.nc + c) for y in range(self.ny) for c in range(self.nc)]
        return lax.ppermute(value, "dp", pairs)

    def swap_core(self, value):
        return lax.ppermute(value, "dp", [(d, d ^ 1) for d in range(self.ny * self.nc)])


def rows_at(value, start, count):
    return lax.dynamic_slice_in_dim(value, start, count, 0)


SMALL = pl.CostEstimate(flops=1000, bytes_accessed=1000, transcendentals=0)


def work(flops):
    return pl.CostEstimate(flops=int(flops), bytes_accessed=1000, transcendentals=0)


PARAMS = pltpu.CompilerParams(vmem_limit_bytes=24 << 20)


def partial_product(rows, weights, starts, size):
    count, (height, width) = len(rows), rows[0].shape

    def kernel(*refs):
        total = jnp.dot(refs[0][...], refs[count][...], preferred_element_type=F32)
        for k in range(1, count):
            total += jnp.dot(refs[k][...], refs[count + k][...], preferred_element_type=F32)
        refs[-1][...] = total.astype(BF16)

    return pl.pallas_call(
        kernel,
        grid=(size // LANES,),
        out_shape=jax.ShapeDtypeStruct((height, size), BF16),
        in_specs=[pl.BlockSpec((height, width), lambda j: (0, 0))] * count
        + [pl.BlockSpec((width, LANES), lambda j, u=s // LANES: (0, u + j)) for s in starts],
        out_specs=pl.BlockSpec((height, LANES), lambda j: (0, j)),
        compiler_params=PARAMS,
        cost_estimate=work(COST * 2 * count * height * width * size),
        name="partial_product",
    )(*rows, *weights)


def return_product(slopes, weights):
    count, height = len(slopes), slopes[0].shape[0]
    sizes = [s.shape[1] for s in slopes]
    width = weights[0].shape[0]
    tile = min(LANES, width)
    places, at = [], 0
    for i, w in enumerate(weights):
        places += [(i, at, c) for c in (0,)]
        at += w.shape[1]

    def columns(refs, start, size):
        for i, first, _ in places:
            if first <= start < first + weights[i].shape[1]:
                return refs[count + i][:, start - first : start - first + size]

    def kernel(*refs):
        total, start = None, 0
        for i, size in enumerate(sizes):
            weight = columns(refs, start, size)
            term = lax.dot_general(refs[i][...], weight, (((1,), (1,)), ((), ())), preferred_element_type=F32)
            total = term if total is None else total + term
            start += size
        refs[-1][...] = total.astype(BF16)

    return pl.pallas_call(
        kernel,
        grid=(width // tile,),
        out_shape=jax.ShapeDtypeStruct((height, width), BF16),
        in_specs=[pl.BlockSpec((height, size), lambda j: (0, 0)) for size in sizes]
        + [pl.BlockSpec((tile, w.shape[1]), lambda j: (j, 0)) for w in weights],
        out_specs=pl.BlockSpec((height, tile), lambda j: (0, j)),
        compiler_params=PARAMS,
        cost_estimate=work(COST * 2 * height * width * sum(sizes)),
        name="return_product",
    )(*slopes, *weights)


def grad_product(half, turned, slopes, extra, kinds):
    groups, count = len(turned), len(slopes)
    height, size = slopes[0].shape
    ny, nc, share, rows = turned[0].shape
    more = 0 if extra is None else groups

    def kernel(half_ref, *refs):
        pieces = refs[groups : groups + count]
        for k in range(groups):
            left = refs[k][...].reshape(ny * share, rows)
            total = None
            for i in range(count):
                term = jnp.dot(left[:, i * height : (i + 1) * height], pieces[i][...], preferred_element_type=F32)
                total = term if total is None else total + term
            total = total.reshape(ny, share, LANES)
            if more:
                total = total + refs[groups + count + k][...].astype(F32)
            out = refs[groups + count + more + k]
            out[...] = total.astype(out.dtype)

    column = pl.BlockSpec((ny, share, LANES), lambda j, h: (0, 0, j))
    return pl.pallas_call(
        kernel,
        grid_spec=pltpu.PrefetchScalarGridSpec(
            num_scalar_prefetch=1,
            grid=(size // LANES,),
            in_specs=[pl.BlockSpec((ny, None, share, rows), lambda j, h: (0, h[0], 0, 0))] * groups
            + [pl.BlockSpec((height, LANES), lambda j, h: (0, j))] * count
            + [column] * more,
            out_specs=[column] * groups,
        ),
        out_shape=[jax.ShapeDtypeStruct((ny, share, size), kind) for kind in kinds],
        compiler_params=PARAMS,
        cost_estimate=work(COST * 2 * groups * ny * share * rows * size),
        name="grad_product",
    )(half, *turned, *slopes, *([] if extra is None else extra))


def place_blocks(out, pieces, owner, offset, taken, me, out_blocks, width):
    where = [(i, j) for i, piece in enumerate(pieces) for j in range(piece.shape[0])]
    count, total = len(pieces), len(where)
    first = out is None

    def kernel(owner_ref, offset_ref, taken_ref, me_ref, *refs):
        sources, (out_ref, stage, zero, in_sems, out_sems, zero_sems) = refs[:count], refs[-6:]
        mine = me_ref[0]

        def arrive(n):
            i, j = where[n]
            return pltpu.make_async_copy(sources[i].at[j], stage.at[n], in_sems.at[n])

        def leave(n):
            return pltpu.make_async_copy(stage.at[n], out_ref.at[offset_ref[n]], out_sems.at[n])

        def clear(n):
            return pltpu.make_async_copy(zero, out_ref.at[n], zero_sems.at[n])

        def each(work):
            for n in range(total):
                pl.when(owner_ref[n] == mine)(lambda: work(n))

        def forward(n):
            arrive(n).wait()
            leave(n).start()

        each(lambda n: arrive(n).start())
        if first:
            zero[...] = jnp.zeros_like(zero)
            for n in range(out_blocks):
                pl.when(taken_ref[n] == 0)(lambda: clear(n).start())
        each(forward)
        each(lambda n: leave(n).wait())
        if first:
            for n in range(out_blocks):
                pl.when(taken_ref[n] == 0)(lambda: clear(n).wait())

    smem = pl.BlockSpec(memory_space=pltpu.SMEM)
    hbm = pl.BlockSpec(memory_space=pl.ANY)
    before = [] if first else [out]
    return pl.pallas_call(
        kernel,
        out_shape=jax.ShapeDtypeStruct((out_blocks, BLOCK, width), BF16),
        in_specs=[smem] * 4 + [hbm] * (count + len(before)),
        out_specs=hbm,
        scratch_shapes=[
            pltpu.VMEM((total, BLOCK, width), BF16),
            pltpu.VMEM((BLOCK, width), BF16),
            pltpu.SemaphoreType.DMA((total,)),
            pltpu.SemaphoreType.DMA((total,)),
            pltpu.SemaphoreType.DMA((out_blocks,)),
        ],
        input_output_aliases={} if first else {4 + count: 0},
        compiler_params=PARAMS,
        cost_estimate=SMALL,
        name="place_blocks",
    )(owner, offset, taken, me, *pieces, *before)


class Order:
    def __init__(self):
        self.last = None

    def pin(self, value):
        if self.last is not None:
            value, _ = lax.optimization_barrier((value, self.last))
        return value

    def done(self, value):
        self.last = value
        return value


def shards(thinker_rows, proj_weight, proj_bias, cotangent, block_owner, block_offset):
    g = Grid(lax.axis_size("tensor"), lax.axis_size("dp"))
    row_count, width = thinker_rows.shape
    dp_count = g.ny * g.nc
    out_width = proj_weight.shape[1]
    x_rows = row_count // g.nx
    x_blocks = x_rows // BLOCK
    nr = min(2, x_blocks)
    r_rows = x_rows // nr
    r_blocks = r_rows // BLOCK
    units = out_width // LANES
    ends = [0] + [round(units * f) * LANES for f in CUTS] + [out_width]
    spans = list(zip(ends[:-1], ends[1:]))
    ne = len(spans)
    loads = [spans[0], spans[1], (spans[2][0], out_width)]
    share = width // dp_count
    xs = range(1, g.nx)
    out_blocks = 2 * row_count // BLOCK
    line = Order()
    later = {}

    def at(tick, work):
        later.setdefault(tick, []).append(work)

    x_weight, x_rows_got = {}, {}

    def load_of(e):
        return min(e, len(loads) - 1)

    def load_weight(i):
        start, end = loads[i]
        mine = lax.dynamic_slice(proj_weight, (line.pin(g.d * share), start), (share, end - start))
        for k in xs:
            x_weight[i, k] = g.swap_x(mine, k)

    def share_far(i):
        for k in xs:
            got = line.pin(x_weight[i, k])
            parts = {ky * g.nc: g.swap_y(got, ky) for ky in range(1, g.ny)}
            parts[0], parts[1] = got, g.swap_core(got)
            x_weight[i, k] = parts

    def share_near(i):
        for k in xs:
            parts = x_weight[i, k]
            for ky in range(1, g.ny):
                key = ky * g.nc
                parts[key] = line.pin(parts[key])
                parts[key + 1] = g.swap_core(parts[key])
            full = jnp.zeros((width, loads[i][1] - loads[i][0]), BF16)
            for key, part in sorted(parts.items()):
                full = lax.dynamic_update_slice(full, part, ((g.d ^ key) * share, 0))
            x_weight[i, k] = line.done(full)

    def share_all(i):
        for k in xs:
            x_weight[i, k] = lax.all_gather(line.pin(x_weight[i, k]), "dp", axis=0, tiled=True)

    def load_rows(r):
        for k in xs:
            mine = rows_at(thinker_rows, (line.pin(g.x) ^ k) * x_rows + r * r_rows, r_rows)
            x_rows_got[r, k] = g.swap_x(mine, k)

    own_rows = [None] * nr
    own_weight = [None] * ne
    turned = {}

    def turn(k, value):
        turned[k] = line.done(value.T.reshape(g.ny, g.nc, share, x_rows))

    def add_up(part, got):
        return line.done((line.pin(part).astype(F32) + got.astype(F32)).astype(BF16))

    partials, hops, slopes = {}, {}, {}

    def partial_of(r, e):
        start, end = spans[e]
        rows = [line.pin(own_rows[r])] + [x_rows_got[r, k] for k in xs]
        i = load_of(e)
        weights = [own_weight[e]] + [x_weight[i, k] for k in xs]
        part = line.done(partial_product(rows, weights, [0] + [start - loads[i][0]] * len(xs), end - start))
        partials[r, e] = part
        hops[r, e] = [g.hop_z(part, 0)]

    def hop(r, e, h):
        hops[r, e].append(g.hop_z(add_up(partials[r, e], hops[r, e][-1]), h))

    def slope_of(r, e):
        start, end = spans[e]
        total = line.pin(partials[r, e]).astype(F32)
        for got in hops[r, e]:
            total = total + got.astype(F32)
        pre_act = total + proj_bias[start:end]
        gate = jax.nn.sigmoid(pre_act)
        cot = lax.dynamic_slice(cotangent, (g.x * x_rows + r * r_rows, start), (r_rows, end - start))
        slopes[r, e] = line.done((cot.astype(F32) * gate * (1.0 + pre_act * (1.0 - gate))).astype(BF16))

    grads = [None] * ne
    half = g.c.astype(jnp.int32)[None]

    def weight_grad(e, tick):
        pieces = [line.pin(slopes[0, e])] + [slopes[r, e] for r in range(1, nr)]
        groups = list(xs) + [0]
        give = grad_product(1 - half, [turned[k] for k in groups], pieces, None, [BF16] * g.nx)
        line.done(give[0])
        got = {k: g.swap_core(v) for k, v in zip(groups, give)}

        def over_x():
            x_got = []
            for k in xs:
                value = grad_product(line.pin(half), [turned[k]], pieces, [got[k]], [BF16])[0]
                x_got.append(g.swap_x(line.done(value), k))
            mine = line.done(grad_product(line.pin(half), [turned[0]], pieces, [got[0]], [F32])[0])

            def over_y():
                total = line.pin(mine)
                for v in x_got:
                    total = total + v.astype(F32)
                total = line.done(total)
                own = lax.dynamic_index_in_dim(total, g.y, 0, keepdims=False)
                y_got = [
                    g.swap_y(lax.dynamic_index_in_dim(total, g.y ^ ky, 0, keepdims=False).astype(BF16), ky)
                    for ky in range(1, g.ny)
                ]

                def finish():
                    value = line.pin(own)
                    for v in y_got:
                        value = value + v.astype(F32)
                    grads[e] = line.done(value * float(row_count * dp_count) ** (-0.5))

                at(tick + 6, finish)

            at(tick + 4, over_y)

        at(tick + 1, over_x)

    state = {"out": None}

    def return_rows(r, tick, gathered):
        grad, placed, placed_at = {}, [], []
        pieces = [slopes[r, e] for e in range(ne)]

        def multiply(k):
            weights = [proj_weight] if k == 0 else [x_weight[i, k] for i in range(len(loads))]
            grad[k] = line.done(return_product([line.pin(pieces[0])] + pieces[1:], weights))

        for k in xs:
            multiply(k)
            grad[k] = g.swap_x(grad[k], k)
        multiply(0)

        def keep_piece(piece, k, ky, kc):
            placed.append(piece.reshape(r_blocks, BLOCK, width))
            placed_at.append((g.d ^ (ky * g.nc + kc), (g.x ^ k) * x_blocks + r * r_blocks))

        def everywhere(k):
            piece = lax.all_gather(line.pin(grad[k]), "dp", axis=0, tiled=True)
            placed.append(piece.reshape(dp_count * r_blocks, BLOCK, width))
            placed_at.extend((s, (g.x ^ k) * x_blocks + r * r_blocks) for s in range(dp_count))

        def spread(k):
            piece = line.pin(grad[k])
            across = [g.swap_y(piece, ky) for ky in range(1, g.ny)]
            keep_piece(piece, k, 0, 0)
            keep_piece(g.swap_core(piece), k, 0, 1)

            def other_core():
                for ky in range(1, g.ny):
                    piece = line.pin(across[ky - 1])
                    keep_piece(piece, k, ky, 0)
                    keep_piece(g.swap_core(piece), k, ky, 1)

            return other_core

        def place():
            sources = jnp.stack(
                [lax.dynamic_slice(tables, (s, 0, t), (1, 2, r_blocks))[0] for s, t in placed_at]
            )
            owner, offset = sources[:, 0].reshape(-1), sources[:, 1].reshape(-1)
            pieces = [line.pin(placed[0])] + placed[1:]
            state["out"] = line.done(
                place_blocks(state["out"], pieces, owner, offset, taken, g.d[None], out_blocks, width)
            )

        if gathered:
            everywhere(0)
            at(tick + 1, lambda: [everywhere(k) for k in xs])
            at(tick + 5, place)
        else:
            own_next = spread(0)

            def after_x():
                for k in xs:
                    at(tick + 3, spread(k))
                at(tick + 4, place)

            at(tick + 1, after_x)
            at(tick + 2, own_next)

    load_weight(0)
    tables = lax.all_gather(jnp.stack([block_owner, block_offset]), "dp", axis=0)
    own_rows[0] = line.done(rows_at(thinker_rows, g.x * x_rows, r_rows))
    load_rows(0)
    mine = line.pin(tables[:, 0]) == g.d
    reached = mine[:, :, None] & (tables[:, 1][:, :, None] == jnp.arange(out_blocks))
    taken = line.done(jnp.any(reached, axis=(0, 1)).astype(jnp.int32))
    share_far(0)
    line.done(x_weight[0, xs[0]][0] if xs else taken)
    for r in range(1, nr):
        load_rows(r)
    for r in range(1, nr):
        own_rows[r] = rows_at(thinker_rows, line.pin(g.x) * x_rows + r * r_rows, r_rows)
    line.done(own_rows[-1])
    turn(0, rows_at(thinker_rows, line.pin(g.x) * x_rows, x_rows))
    own_weight[0] = line.done(line.pin(proj_weight[:, spans[0][0] : spans[0][1]]))
    share_near(0)

    chunks = [(r, 0) for r in range(nr)] + [(0, e) for e in range(1, ne)]
    chunks += [(r, e) for r in range(1, nr) for e in range(1, ne)]
    before = {
        1: [lambda: share_near(1)],
        2: [lambda: share_near(2)],
        3: [
            lambda: [
                turn(k, jnp.concatenate([line.pin(x_rows_got[0, k])] + [x_rows_got[r, k] for r in range(1, nr)], axis=0))
                for k in xs
            ]
        ],
    }

    def own_columns(e):
        own_weight[e] = line.done(line.pin(proj_weight[:, spans[e][0] : spans[e][1]]))

    at(0, lambda: load_weight(2))
    at(0, lambda: own_columns(1))
    at(0, lambda: share_far(1))
    at(1, lambda: share_far(2))
    at(1, lambda: [own_columns(e) for e in range(2, ne)])
    partial_of(*chunks[0])
    load_weight(1)
    tick = 0
    hop_count = g.nz - 1

    def hop_all():
        for h in range(1, hop_count):
            if 0 <= tick - h + 1 < len(chunks):
                hop(*chunks[tick - h + 1], h)

    while tick < len(chunks) + hop_count or any(t >= tick for t in later):
        early = False
        if early:
            hop_all()
        for work in before.get(tick, []):
            work()
        if tick + 1 < len(chunks):
            partial_of(*chunks[tick + 1])
        if not early:
            hop_all()
        ready = tick - hop_count + 1
        if 0 <= ready < len(chunks):
            r, e = chunks[ready]
            slope_of(r, e)
            if all((r, j) in slopes for j in range(ne)):
                return_rows(r, tick, r < GATHERED)
            if all((j, e) in slopes for j in range(nr)):
                weight_grad(e, tick)
        for work in later.pop(tick, []):
            work()
        tick += 1

    return state["out"].reshape(out_blocks * BLOCK, width), jnp.concatenate(grads, axis=1)


def solution(mesh):
    return jax.shard_map(
        shards,
        mesh=mesh,
        in_specs=(P("dp", "tensor"), P("tensor", None), P(), P("dp", None), P("dp"), P("dp")),
        out_specs=(P("dp", "tensor"), P(("tensor", "dp"), None)),
        check_vma=False,
    )
```

time: 689 us -> 492 us (0.71)
  the two profiles are of different devices: /device:TPU:0 before, /device:TPU:8 now
where the time goes in v2:
time: 492 us; the launch traced here: 482 us
  waiting for transfers between devices  160 us (33%)
  Pallas kernels  89.7 us (18%)
  starting transfers between devices  83.1 us (17%)
  local copies, waits for them, and re-layouts  64.6 us (13%)
  other arithmetic  63.5 us (13%)
  between operations  16.1 us (3%)
  blocking collectives  5.07 us (1%)
    ppermute x11, waiting for transfers between devices, swap_x(): return lax.ppermute(value, 'tensor', pairs)  79.4 us
    ppermute x24, starting transfers between devices, hop_z(): return lax.ppermute(value, 'tensor', pairs)  58 us
    ppermute x24, waiting for transfers between devices, hop_z(): return lax.ppermute(value, 'tensor', pairs)  46.5 us
    ppermute x9, waiting for transfers between devices, swap_y(): return lax.ppermute(value, 'dp', pairs)  34 us
    pallas_call x12, Pallas kernels, grad_product(): pl.pallas_call(kernel, grid_spec=pltpu.PrefetchScalarGridSpec(num_scalar_...  33.2 us
    pallas_call x8, Pallas kernels, partial_product(): pl.pallas_call(kernel, grid=(size // LANES,), out_shape=jax.ShapeDtypeStr...  30.1 us
    convert_element_type x16, other arithmetic, add_up(): (line.pin(part).astype(F32) + got.astype(F32)).astype(BF16)  24.4 us
    convert_element_type x8, other arithmetic, slope_of(): (cot.astype(F32) * gate * (1.0 + pre_act * (1.0 - gate))).astype(BF16)  24.3 us
  transfers between devices with their start and end apart: 64, of which 21 were waited for; matrix products, arithmetic and copies ran while one was open for 21% of the time, Pallas kernels for 17%

profile of v2, /device:TPU:8, one launch (start us, length us, event | category | flops | bytes accessed | tf_op | source)
XLA Modules:
  0.0 482.2 jit_solution(3045584951004296139)
XLA Ops:
  11.2 5.1 %all-gather.1 = s32[4,2,16]{2,1,0:T(2,128)S(1)} all-gather(s32[1,2,16]{2,1,0:T(2,128)S(1)} %add_bitcast_fusion), channel_id=2, replica_groups=mesh['dp'=4,'tensor'=8] {'dp'}, dimensions={0}, use_global_device_ids=true | all-gather | bytes 640 | tf_op jit(solution)/shard_map/all_gather | solution.py:431
  16.4 5.7 %collective-permute-done = bf16[256,1024]{1,0:T(8,128)(2,1)} collective-permute-done((bf16[256,1024]{1,0:T(8,128)(2,1)S(1)}, bf16[256,1024]{1,0:T(8,128)(2,1)}, u32[]{:S(2)}, u32[]{:S(2)}) %collective-permute-start) | collective-permute-done | bytes 524320 | tf_op jit(solution)/shard_map/ppermute | solution.py:30
  23.7 3.6 constant_dynamic-slice_fusion.8
  28.8 4.7 fusion.39
  36.5 4.0 copy.15
  46.2 7.3 %collective-permute-done.4.refs_1_ = bf16[512,1024]{1,0:T(8,128)(2,1)S(1)} collective-permute-done((bf16[512,1024]{1,0:T(8,128)(2,1)}, bf16[512,1024]{1,0:T(8,128)(2,1)S(1)}, u32[]{:S(2)}, u32[]{:S(2)}) %collective-permute-start.4) | collective-permute-done | bytes 1048608 | tf_op jit(solution)/shard_map/ppermute | solution.py:30
  55.7 3.5 partial_product.8
  63.3 12.8 %collective-permute-done.5.refs_1_ = bf16[512,1024]{1,0:T(8,128)(2,1)} collective-permute-done((bf16[512,1024]{1,0:T(8,128)(2,1)}, bf16[512,1024]{1,0:T(8,128)(2,1)}, u32[]{:S(2)}, u32[]{:S(2)}) %collective-permute-start.5) | collective-permute-done | bytes 1048608 | tf_op jit(solution)/shard_map/ppermute | solution.py:30
  79.2 4.6 partial_product.9
  90.0 3.5 collective-permute-start.13
  93.5 7.2 %collective-permute-done.9 = bf16[256,1024]{1,0:T(8,128)(2,1)S(1)} collective-permute-done((bf16[256,1024]{1,0:T(8,128)(2,1)}, bf16[256,1024]{1,0:T(8,128)(2,1)S(1)}, u32[]{:S(2)}, u32[]{:S(2)}) %collective-permute-start.9) | collective-permute-done | bytes 524320 | tf_op jit(solution)/shard_map/ppermute | solution.py:39
  106.2 3.5 partial_product.10
  109.7 6.6 %collective-permute-done.12 = bf16[512,1024]{1,0:T(8,128)(2,1)} collective-permute-done((bf16[512,1024]{1,0:T(8,128)(2,1)S(1)}, bf16[512,1024]{1,0:T(8,128)(2,1)}, u32[]{:S(2)}, u32[]{:S(2)}) %collective-permute-start.12) | collective-permute-done | bytes 1048608 | tf_op jit(solution)/shard_map/ppermute | solution.py:35
  123.0 3.7 fusion.38
  126.8 14.8 %collective-permute-done.15 = bf16[256,1536]{1,0:T(8,128)(2,1)} collective-permute-done((bf16[256,1536]{1,0:T(8,128)(2,1)}, bf16[256,1536]{1,0:T(8,128)(2,1)}, u32[]{:S(2)}, u32[]{:S(2)}) %collective-permute-start.15) | collective-permute-done | bytes 786464 | tf_op jit(solution)/shard_map/ppermute | solution.py:39
  142.9 3.5 collective-permute-start.18
  153.6 3.3 partial_product.11
  158.1 11.3 %collective-permute-done.17 = bf16[512,1024]{1,0:T(8,128)(2,1)S(1)} collective-permute-done((bf16[512,1024]{1,0:T(8,128)(2,1)S(1)}, bf16[512,1024]{1,0:T(8,128)(2,1)S(1)}, u32[]{:S(2)}, u32[]{:S(2)}) %collective-permute-start.17) | collective-permute-done | bytes 1048608 | tf_op jit(solution)/shard_map/ppermute | solution.py:35
  170.8 3.5 collective-permute-start.21
  178.3 4.2 multiply_convert_fusion.3.refs_2_.refs_1_.refs_0_
  185.2 4.0 copy.16
  203.2 3.3 collective-permute-start.25
  209.8 3.6 grad_product.12
  213.5 4.6 partial_product.13
  223.9 3.9 collective-permute-done.25
  227.8 4.4 collective-permute-start.30
  241.2 4.3 partial_product.14
  255.7 3.8 partial_product.15
  259.5 4.8 %collective-permute-done.31 = bf16[512,768]{1,0:T(8,128)(2,1)S(1)} collective-permute-done((bf16[512,768]{1,0:T(8,128)(2,1)S(1)}, bf16[512,768]{1,0:T(8,128)(2,1)S(1)}, u32[]{:S(2)}, u32[]{:S(2)}) %collective-permute-start.31) | collective-permute-done | bytes 786464 | tf_op jit(solution)/shard_map/ppermute | solution.py:35
  265.5 7.2 %collective-permute-done.32 = bf16[512,1024]{1,0:T(8,128)(2,1)S(1)} collective-permute-done((bf16[512,1024]{1,0:T(8,128)(2,1)S(1)}, bf16[512,1024]{1,0:T(8,128)(2,1)S(1)}, u32[]{:S(2)}, u32[]{:S(2)}) %collective-permute-start.32) | collective-permute-done | bytes 1048608 | tf_op jit(solution)/shard_map/ppermute | solution.py:35
  276.5 4.7 return_product.4
  282.3 4.7 return_product.5
  292.2 5.5 %collective-permute-start.36 = (bf16[512,1024]{1,0:T(8,128)(2,1)}, bf16[512,1024]{1,0:T(8,128)(2,1)}, u32[]{:S(2)}, u32[]{:S(2)}) collective-permute-start(bf16[512,1024]{1,0:T(8,128)(2,1)} %fusion.13), channel_id=1, source_target_pairs={{4,6},{5,7},{2,0},{3,1},{12,14},{13,15},{10,8},{11,9},{20,22},{21,... | collective-permute-start | bytes 3145736 | tf_op jit(solution)/shard_map/ppermute | solution.py:35
  300.3 7.1 %collective-permute-done.34 = bf16[512,768]{1,0:T(8,128)(2,1)} collective-permute-done((bf16[512,768]{1,0:T(8,128)(2,1)S(1)}, bf16[512,768]{1,0:T(8,128)(2,1)}, u32[]{:S(2)}, u32[]{:S(2)}) %collective-permute-start.34) | collective-permute-done | bytes 786464 | tf_op jit(solution)/shard_map/ppermute | solution.py:35
  316.8 3.8 collective-permute-done.36
  323.5 4.2 grad_product.15
  329.5 13.8 %collective-permute-done.48 = bf16[512,1024]{1,0:T(8,128)(2,1)} collective-permute-done((bf16[512,1024]{1,0:T(8,128)(2,1)}, bf16[512,1024]{1,0:T(8,128)(2,1)}, u32[]{:S(2)}, u32[]{:S(2)}) %collective-permute-start.48) | collective-permute-done | bytes 1048608 | tf_op jit(solution)/shard_map/ppermute | solution.py:30
  347.7 3.4 multiply_convert_fusion.5.refs_3_.refs_2_
  354.3 4.4 grad_product.17
  365.5 4.7 return_product.6
  371.7 5.4 %return_product.7 = bf16[512,1024]{1,0:T(8,128)(2,1)} custom-call(bf16[512,1024]{1,0:T(8,128)(2,1)S(1)} %copy-done.37, bf16[512,1024]{1,0:T(8,128)(2,1)S(1)} %copy-done.50, bf16[512,768]{1,0:T(8,128)(2,1)S(1)} %multiply_convert_fusion.5.refs_3_.refs_2_, bf16[512,768]{1,0:T(8,128)(2,1)S(1)} %multiply_convert_fusion.4.refs_3_.refs_2_, ...), custom_call_target="tpu_custom_call" | custom-call | flops 11274289152 | bytes 1000 | tf_op jit(solution)/shard_map/return_product/pallas_call | solution.py:105
  387.0 9.3 %collective-permute-done.52 = bf16[512,1024]{1,0:T(8,128)(2,1)} collective-permute-done((bf16[512,1024]{1,0:T(8,128)(2,1)S(1)}, bf16[512,1024]{1,0:T(8,128)(2,1)}, u32[]{:S(2)}, u32[]{:S(2)}) %collective-permute-start.52) | collective-permute-done | bytes 1048608 | tf_op jit(solution)/shard_map/ppermute | solution.py:30
  407.3 5.1 %place_blocks.2.refs_8_ = bf16[32,128,1024]{2,1,0:T(8,128)(2,1)} custom-call(s32[32]{0:T(128)S(1)} %reshape_squeeze.14.owner_ref, s32[32]{0:T(128)S(1)} %reshape_squeeze.15.offset_ref, s32[32]{0:T(128)S(1)} %convert_element_type.307.taken_ref, s32[1]{0:T(128)} %bitcast.5.me_ref, bf16[16,128,1024]{2,1,0:T(8,128)(2,1)S(1)} %bitcast.45, ...), custom_call_target="tpu_custom_call" | custom-call | flops 1000 | bytes 1000 | tf_op jit(solution)/shard_map/place_blocks/pallas_call | solution.py:197
  412.5 6.3 %collective-permute-done.49 = bf16[2,256,1024]{2,1,0:T(8,128)(2,1)} collective-permute-done((bf16[2,256,1024]{2,1,0:T(8,128)(2,1)}, bf16[2,256,1024]{2,1,0:T(8,128)(2,1)}, u32[]{:S(2)}, u32[]{:S(2)}) %collective-permute-start.49) | collective-permute-done | bytes 1048608 | tf_op jit(solution)/shard_map/ppermute | solution.py:30
  421.6 13.3 %collective-permute-done.50 = bf16[2,256,768]{2,1,0:T(8,128)(2,1)} collective-permute-done((bf16[2,256,768]{2,1,0:T(8,128)(2,1)}, bf16[2,256,768]{2,1,0:T(8,128)(2,1)}, u32[]{:S(2)}, u32[]{:S(2)}) %collective-permute-start.50) | collective-permute-done | bytes 786464 | tf_op jit(solution)/shard_map/ppermute | solution.py:30
  447.4 10.3 %collective-permute-done.58 = bf16[2,256,768]{2,1,0:T(8,128)(2,1)} collective-permute-done((bf16[2,256,768]{2,1,0:T(8,128)(2,1)}, bf16[2,256,768]{2,1,0:T(8,128)(2,1)}, u32[]{:S(2)}, u32[]{:S(2)}) %collective-permute-start.58) | collective-permute-done | bytes 786464 | tf_op jit(solution)/shard_map/ppermute | solution.py:30
  460.5 4.9 %collective-permute-done.60 = bf16[256,768]{1,0:T(8,128)(2,1)S(1)} collective-permute-done((bf16[256,768]{1,0:T(8,128)(2,1)S(1)}, bf16[256,768]{1,0:T(8,128)(2,1)S(1)}, u32[]{:S(2)}, u32[]{:S(2)}) %collective-permute-start.60) | collective-permute-done | bytes 393248 | tf_op jit(solution)/shard_map/ppermute | solution.py:39
  465.5 7.1 %collective-permute-done.61 = bf16[256,768]{1,0:T(8,128)(2,1)S(1)} collective-permute-done((bf16[256,768]{1,0:T(8,128)(2,1)S(1)}, bf16[256,768]{1,0:T(8,128)(2,1)S(1)}, u32[]{:S(2)}, u32[]{:S(2)}) %collective-permute-start.61) | collective-permute-done | bytes 393248 | tf_op jit(solution)/shard_map/ppermute | solution.py:39
  (352 shorter events, 187.7 us)
Async XLA Ops:
  7.2 395.7 %all-gather.5.cloned.1.call-start = ((), (), s32[]{:S(2)}) async-start(), calls=%async_computation | async-start | bytes 5242880 | tf_op jit(solution)/shard_map/all_gather | solution.py:387
  23.7 19.2 %collective-permute-start.1 = (bf16[256,1024]{1,0:T(8,128)(2,1)}, bf16[256,1024]{1,0:T(8,128)(2,1)}, u32[]{:S(2)}, u32[]{:S(2)}) collective-permute-start(bf16[256,1024]{1,0:T(8,128)(2,1)} %collective-permute-done), channel_id=1, source_target_pairs={{0,8},{8,0},{16,24},{24,16},{1,9},{9,1},{17,25},{25,17},{2,10},{10... | collective-permute-start | bytes 1572872 | tf_op jit(solution)/shard_map/ppermute | solution.py:42
  27.3 26.2 %collective-permute-start.4 = (bf16[512,1024]{1,0:T(8,128)(2,1)}, bf16[512,1024]{1,0:T(8,128)(2,1)S(1)}, u32[]{:S(2)}, u32[]{:S(2)}) collective-permute-start(bf16[512,1024]{1,0:T(8,128)(2,1)} %get-tuple-element.190), channel_id=1, source_target_pairs={{0,1},{1,0},{2,3},{3,2},{4,5},{5,4},{6,7},{7,6},{8,9},{9,8},{10,11... | collective-permute-start | bytes 3145736 | tf_op jit(solution)/shard_map/ppermute | solution.py:30
  40.7 35.3 %collective-permute-start.5 = (bf16[512,1024]{1,0:T(8,128)(2,1)}, bf16[512,1024]{1,0:T(8,128)(2,1)}, u32[]{:S(2)}, u32[]{:S(2)}) collective-permute-start(bf16[512,1024]{1,0:T(8,128)(2,1)} %get-tuple-element.188), channel_id=1, source_target_pairs={{0,1},{1,0},{2,3},{3,2},{4,5},{5,4},{6,7},{7,6},{8,9},{9,8},{10,11... | collective-permute-start | bytes 3145736 | tf_op jit(solution)/shard_map/ppermute | solution.py:30
  59.2 26.4 %collective-permute-start.7 = (bf16[512,1024]{1,0:T(8,128)(2,1)S(1)}, bf16[512,1024]{1,0:T(8,128)(2,1)}, u32[]{:S(2)}, u32[]{:S(2)}) collective-permute-start(bf16[512,1024]{1,0:T(8,128)(2,1)S(1)} %partial_product.8), channel_id=1, source_target_pairs={{0,2},{1,3},{6,4},{7,5},{8,10},{9,11},{14,12},{15,13},{16,18},{17,... | collective-permute-start | bytes 3145736 | tf_op jit(solution)/shard_map/ppermute | solution.py:35
  61.7 26.5 %collective-permute-start.6 = (bf16[256,1024]{1,0:T(8,128)(2,1)S(1)}, bf16[256,1024]{1,0:T(8,128)(2,1)}, u32[]{:S(2)}, u32[]{:S(2)}) collective-permute-start(bf16[256,1024]{1,0:T(8,128)(2,1)S(1)} %constant_dynamic-slice_fusion.22), channel_id=1, source_target_pairs={{0,1},{1,0},{2,3},{3,2},{4,5},{5,4},{6,7},{7,6},{8,9},{9,8},{10,11... | collective-permute-start | bytes 1572872 | tf_op jit(solution)/shard_map/ppermute | solution.py:30
  88.7 27.6 %collective-permute-start.12 = (bf16[512,1024]{1,0:T(8,128)(2,1)S(1)}, bf16[512,1024]{1,0:T(8,128)(2,1)}, u32[]{:S(2)}, u32[]{:S(2)}) collective-permute-start(bf16[512,1024]{1,0:T(8,128)(2,1)S(1)} %partial_product.9), channel_id=1, source_target_pairs={{0,2},{1,3},{6,4},{7,5},{8,10},{9,11},{14,12},{15,13},{16,18},{17,... | collective-permute-start | bytes 3145736 | tf_op jit(solution)/shard_map/ppermute | solution.py:35
  90.0 28.9 %collective-permute-start.13 = (bf16[512,1024]{1,0:T(8,128)(2,1)}, bf16[512,1024]{1,0:T(8,128)(2,1)}, u32[]{:S(2)}, u32[]{:S(2)}) collective-permute-start(bf16[512,1024]{1,0:T(8,128)(2,1)} %fusion), channel_id=1, source_target_pairs={{2,4},{3,5},{4,2},{5,3},{10,12},{11,13},{12,10},{13,11},{18,20},{1... | collective-permute-start | bytes 3145736 | tf_op jit(solution)/shard_map/ppermute | solution.py:35
  102.0 20.1 %collective-permute-start.11 = (bf16[256,1536]{1,0:T(8,128)(2,1)S(1)}, bf16[256,1536]{1,0:T(8,128)(2,1)}, u32[]{:S(2)}, u32[]{:S(2)}) collective-permute-start(bf16[256,1536]{1,0:T(8,128)(2,1)S(1)} %constant_dynamic-slice_fusion.21), channel_id=1, source_target_pairs={{0,1},{1,0},{2,3},{3,2},{4,5},{5,4},{6,7},{7,6},{8,9},{9,8},{10,11... | collective-permute-start | bytes 2359304 | tf_op jit(solution)/shard_map/ppermute | solution.py:30
  122.1 19.5 %collective-permute-start.15 = (bf16[256,1536]{1,0:T(8,128)(2,1)}, bf16[256,1536]{1,0:T(8,128)(2,1)}, u32[]{:S(2)}, u32[]{:S(2)}) collective-permute-start(bf16[256,1536]{1,0:T(8,128)(2,1)} %collective-permute-done.11), channel_id=1, source_target_pairs={{0,16},{8,24},{16,0},{24,8},{1,17},{9,25},{17,1},{25,9},{2,18},{10... | collective-permute-start | bytes 2359304 | tf_op jit(solution)/shard_map/ppermute | solution.py:39
  123.0 26.7 %collective-permute-start.14 = (bf16[256,1536]{1,0:T(8,128)(2,1)}, bf16[256,1536]{1,0:T(8,128)(2,1)}, u32[]{:S(2)}, u32[]{:S(2)}) collective-permute-start(bf16[256,1536]{1,0:T(8,128)(2,1)} %collective-permute-done.11), channel_id=1, source_target_pairs={{0,8},{8,0},{16,24},{24,16},{1,9},{9,1},{17,25},{25,17},{2,10},{10... | collective-permute-start | bytes 2359304 | tf_op jit(solution)/shard_map/ppermute | solution.py:42
  141.6 27.8 %collective-permute-start.17 = (bf16[512,1024]{1,0:T(8,128)(2,1)S(1)}, bf16[512,1024]{1,0:T(8,128)(2,1)S(1)}, u32[]{:S(2)}, u32[]{:S(2)}) collective-permute-start(bf16[512,1024]{1,0:T(8,128)(2,1)S(1)} %partial_product.10), channel_id=1, source_target_pairs={{0,2},{1,3},{6,4},{7,5},{8,10},{9,11},{14,12},{15,13},{16,18},{17,... | collective-permute-start | bytes 3145736 | tf_op jit(solution)/shard_map/ppermute | solution.py:35
  142.9 31.4 %collective-permute-start.18 = (bf16[512,1024]{1,0:T(8,128)(2,1)}, bf16[512,1024]{1,0:T(8,128)(2,1)S(1)}, u32[]{:S(2)}, u32[]{:S(2)}) collective-permute-start(bf16[512,1024]{1,0:T(8,128)(2,1)} %fusion.1), channel_id=1, source_target_pairs={{2,4},{3,5},{4,2},{5,3},{10,12},{11,13},{12,10},{13,11},{18,20},{1... | collective-permute-start | bytes 3145736 | tf_op jit(solution)/shard_map/ppermute | solution.py:35
  146.4 31.8 %collective-permute-start.19 = (bf16[512,1024]{1,0:T(8,128)(2,1)}, bf16[512,1024]{1,0:T(8,128)(2,1)S(1)}, u32[]{:S(2)}, u32[]{:S(2)}) collective-permute-start(bf16[512,1024]{1,0:T(8,128)(2,1)} %fusion.2), channel_id=1, source_target_pairs={{4,6},{5,7},{2,0},{3,1},{12,14},{13,15},{10,8},{11,9},{20,22},{21,... | collective-permute-start | bytes 3145736 | tf_op jit(solution)/shard_map/ppermute | solution.py:35
  156.8 40.6 %collective-permute-start.20 = (bf16[512,768]{1,0:T(8,128)(2,1)}, bf16[512,768]{1,0:T(8,128)(2,1)}, u32[]{:S(2)}, u32[]{:S(2)}) collective-permute-start(bf16[512,768]{1,0:T(8,128)(2,1)} %partial_product.11), channel_id=1, source_target_pairs={{0,2},{1,3},{6,4},{7,5},{8,10},{9,11},{14,12},{15,13},{16,18},{17,... | collective-permute-start | bytes 2359304 | tf_op jit(solution)/shard_map/ppermute | solution.py:35
  170.8 30.7 %collective-permute-start.21 = (bf16[512,1024]{1,0:T(8,128)(2,1)}, bf16[512,1024]{1,0:T(8,128)(2,1)}, u32[]{:S(2)}, u32[]{:S(2)}) collective-permute-start(bf16[512,1024]{1,0:T(8,128)(2,1)} %fusion.5), channel_id=1, source_target_pairs={{2,4},{3,5},{4,2},{5,3},{10,12},{11,13},{12,10},{13,11},{18,20},{1... | collective-permute-start | bytes 3145736 | tf_op jit(solution)/shard_map/ppermute | solution.py:35
  175.7 30.8 %collective-permute-start.22 = (bf16[512,1024]{1,0:T(8,128)(2,1)}, bf16[512,1024]{1,0:T(8,128)(2,1)}, u32[]{:S(2)}, u32[]{:S(2)}) collective-permute-start(bf16[512,1024]{1,0:T(8,128)(2,1)} %fusion.6), channel_id=1, source_target_pairs={{4,6},{5,7},{2,0},{3,1},{12,14},{13,15},{10,8},{11,9},{20,22},{21,... | collective-permute-start | bytes 3145736 | tf_op jit(solution)/shard_map/ppermute | solution.py:35
  196.2 23.5 %collective-permute-start.23 = (bf16[512,768]{1,0:T(8,128)(2,1)S(1)}, bf16[512,768]{1,0:T(8,128)(2,1)S(1)}, u32[]{:S(2)}, u32[]{:S(2)}) collective-permute-start(bf16[512,768]{1,0:T(8,128)(2,1)S(1)} %partial_product.12), channel_id=1, source_target_pairs={{0,2},{1,3},{6,4},{7,5},{8,10},{9,11},{14,12},{15,13},{16,18},{17,... | collective-permute-start | bytes 2359304 | tf_op jit(solution)/shard_map/ppermute | solution.py:35
  199.0 23.3 %collective-permute-start.24 = (bf16[512,768]{1,0:T(8,128)(2,1)S(1)}, bf16[512,768]{1,0:T(8,128)(2,1)S(1)}, u32[]{:S(2)}, u32[]{:S(2)}) collective-permute-start(bf16[512,768]{1,0:T(8,128)(2,1)S(1)} %fusion.16), channel_id=1, source_target_pairs={{2,4},{3,5},{4,2},{5,3},{10,12},{11,13},{12,10},{13,11},{18,20},{1... | collective-permute-start | bytes 2359304 | tf_op jit(solution)/shard_map/ppermute | solution.py:35
  203.2 24.6 %collective-permute-start.25 = (bf16[512,1024]{1,0:T(8,128)(2,1)S(1)}, bf16[512,1024]{1,0:T(8,128)(2,1)S(1)}, u32[]{:S(2)}, u32[]{:S(2)}) collective-permute-start(bf16[512,1024]{1,0:T(8,128)(2,1)S(1)} %fusion.9), channel_id=1, source_target_pairs={{4,6},{5,7},{2,0},{3,1},{12,14},{13,15},{10,8},{11,9},{20,22},{21,... | collective-permute-start | bytes 3145736 | tf_op jit(solution)/shard_map/ppermute | solution.py:35
  213.4 21.7 %collective-permute-start.26 = (bf16[2,256,1024]{2,1,0:T(8,128)(2,1)S(1)}, bf16[2,256,1024]{2,1,0:T(8,128)(2,1)S(1)}, u32[]{:S(2)}, u32[]{:S(2)}) collective-permute-start(bf16[2,256,1024]{2,1,0:T(8,128)(2,1)S(1)} %get-tuple-element.123), channel_id=1, source_target_pairs={{0,8},{8,0},{16,24},{24,16},{1,9},{9,1},{17,25},{25,17},{2,10},{10... | collective-permute-start | bytes 3145736 | tf_op jit(solution)/shard_map/ppermute | solution.py:42
  218.2 28.6 %collective-permute-start.28 = (bf16[512,1024]{1,0:T(8,128)(2,1)S(1)}, bf16[512,1024]{1,0:T(8,128)(2,1)S(1)}, u32[]{:S(2)}, u32[]{:S(2)}) collective-permute-start(bf16[512,1024]{1,0:T(8,128)(2,1)S(1)} %partial_product.13), channel_id=1, source_target_pairs={{0,2},{1,3},{6,4},{7,5},{8,10},{9,11},{14,12},{15,13},{16,18},{17,... | collective-permute-start | bytes 3145736 | tf_op jit(solution)/shard_map/ppermute | solution.py:35
  219.8 29.8 %collective-permute-start.29 = (bf16[512,768]{1,0:T(8,128)(2,1)S(1)}, bf16[512,768]{1,0:T(8,128)(2,1)S(1)}, u32[]{:S(2)}, u32[]{:S(2)}) collective-permute-start(bf16[512,768]{1,0:T(8,128)(2,1)S(1)} %fusion.17), channel_id=1, source_target_pairs={{2,4},{3,5},{4,2},{5,3},{10,12},{11,13},{12,10},{13,11},{18,20},{1... | collective-permute-start | bytes 2359304 | tf_op jit(solution)/shard_map/ppermute | solution.py:35
  227.8 25.2 %collective-permute-start.30 = (bf16[512,768]{1,0:T(8,128)(2,1)S(1)}, bf16[512,768]{1,0:T(8,128)(2,1)S(1)}, u32[]{:S(2)}, u32[]{:S(2)}) collective-permute-start(bf16[512,768]{1,0:T(8,128)(2,1)S(1)} %fusion.18), channel_id=1, source_target_pairs={{4,6},{5,7},{2,0},{3,1},{12,14},{13,15},{10,8},{11,9},{20,22},{21,... | collective-permute-start | bytes 2359304 | tf_op jit(solution)/shard_map/ppermute | solution.py:35
  247.2 25.6 %collective-permute-start.32 = (bf16[512,1024]{1,0:T(8,128)(2,1)S(1)}, bf16[512,1024]{1,0:T(8,128)(2,1)S(1)}, u32[]{:S(2)}, u32[]{:S(2)}) collective-permute-start(bf16[512,1024]{1,0:T(8,128)(2,1)S(1)} %fusion.12), channel_id=1, source_target_pairs={{2,4},{3,5},{4,2},{5,3},{10,12},{11,13},{12,10},{13,11},{18,20},{1... | collective-permute-start | bytes 3145736 | tf_op jit(solution)/shard_map/ppermute | solution.py:35
  249.9 24.3 %collective-permute-start.33 = (bf16[512,768]{1,0:T(8,128)(2,1)S(1)}, bf16[512,768]{1,0:T(8,128)(2,1)S(1)}, u32[]{:S(2)}, u32[]{:S(2)}) collective-permute-start(bf16[512,768]{1,0:T(8,128)(2,1)S(1)} %fusion.21), channel_id=1, source_target_pairs={{4,6},{5,7},{2,0},{3,1},{12,14},{13,15},{10,8},{11,9},{20,22},{21,... | collective-permute-start | bytes 2359304 | tf_op jit(solution)/shard_map/ppermute | solution.py:35
  288.0 115.0 %all-gather.7.cloned.1.call-start = ((), (), s32[]{:S(2)}) async-start(), calls=%async_computation.1 | async-start | bytes 5242880 | tf_op jit(solution)/shard_map/all_gather | solution.py:387
  288.2 19.2 %collective-permute-start.34 = (bf16[512,768]{1,0:T(8,128)(2,1)S(1)}, bf16[512,768]{1,0:T(8,128)(2,1)}, u32[]{:S(2)}, u32[]{:S(2)}) collective-permute-start(bf16[512,768]{1,0:T(8,128)(2,1)S(1)} %partial_product.15), channel_id=1, source_target_pairs={{0,2},{1,3},{6,4},{7,5},{8,10},{9,11},{14,12},{15,13},{16,18},{17,... | collective-permute-start | bytes 2359304 | tf_op jit(solution)/shard_map/ppermute | solution.py:35
  289.7 22.4 %collective-permute-start.35 = (bf16[512,768]{1,0:T(8,128)(2,1)}, bf16[512,768]{1,0:T(8,128)(2,1)}, u32[]{:S(2)}, u32[]{:S(2)}) collective-permute-start(bf16[512,768]{1,0:T(8,128)(2,1)} %fusion.24), channel_id=1, source_target_pairs={{2,4},{3,5},{4,2},{5,3},{10,12},{11,13},{12,10},{13,11},{18,20},{1... | collective-permute-start | bytes 2359304 | tf_op jit(solution)/shard_map/ppermute | solution.py:35
  292.2 28.4 %collective-permute-start.36 = (bf16[512,1024]{1,0:T(8,128)(2,1)}, bf16[512,1024]{1,0:T(8,128)(2,1)}, u32[]{:S(2)}, u32[]{:S(2)}) collective-permute-start(bf16[512,1024]{1,0:T(8,128)(2,1)} %fusion.13), channel_id=1, source_target_pairs={{4,6},{5,7},{2,0},{3,1},{12,14},{13,15},{10,8},{11,9},{20,22},{21,... | collective-permute-start | bytes 3145736 | tf_op jit(solution)/shard_map/ppermute | solution.py:35
  298.2 29.5 %collective-permute-start.37 = (bf16[2,256,1024]{2,1,0:T(8,128)(2,1)}, bf16[2,256,1024]{2,1,0:T(8,128)(2,1)S(1)}, u32[]{:S(2)}, u32[]{:S(2)}) collective-permute-start(bf16[2,256,1024]{2,1,0:T(8,128)(2,1)} %copy-done.55), channel_id=1, source_target_pairs={{0,1},{1,0},{2,3},{3,2},{4,5},{5,4},{6,7},{7,6},{8,9},{9,8},{10,11... | collective-permute-start | bytes 3145736 | tf_op jit(solution)/shard_map/ppermute | solution.py:30
  299.8 43.5 %collective-permute-start.48 = (bf16[512,1024]{1,0:T(8,128)(2,1)}, bf16[512,1024]{1,0:T(8,128)(2,1)}, u32[]{:S(2)}, u32[]{:S(2)}) collective-permute-start(bf16[512,1024]{1,0:T(8,128)(2,1)} %copy-done.56), channel_id=1, source_target_pairs={{0,1},{1,0},{2,3},{3,2},{4,5},{5,4},{6,7},{7,6},{8,9},{9,8},{10,11... | collective-permute-start | bytes 3145736 | tf_op jit(solution)/shard_map/ppermute | solution.py:30
  309.6 33.8 %collective-permute-start.38 = (bf16[512,768]{1,0:T(8,128)(2,1)}, bf16[512,768]{1,0:T(8,128)(2,1)}, u32[]{:S(2)}, u32[]{:S(2)}) collective-permute-start(bf16[512,768]{1,0:T(8,128)(2,1)} %fusion.25), channel_id=1, source_target_pairs={{2,4},{3,5},{4,2},{5,3},{10,12},{11,13},{12,10},{13,11},{18,20},{1... | collective-permute-start | bytes 2359304 | tf_op jit(solution)/shard_map/ppermute | solution.py:35
  314.3 33.3 %collective-permute-start.39 = (bf16[512,768]{1,0:T(8,128)(2,1)}, bf16[512,768]{1,0:T(8,128)(2,1)}, u32[]{:S(2)}, u32[]{:S(2)}) collective-permute-start(bf16[512,768]{1,0:T(8,128)(2,1)} %fusion.26), channel_id=1, source_target_pairs={{4,6},{5,7},{2,0},{3,1},{12,14},{13,15},{10,8},{11,9},{20,22},{21,... | collective-permute-start | bytes 2359304 | tf_op jit(solution)/shard_map/ppermute | solution.py:35
  327.7 26.3 %collective-permute-start.40 = (bf16[2,256,1024]{2,1,0:T(8,128)(2,1)}, bf16[2,256,1024]{2,1,0:T(8,128)(2,1)}, u32[]{:S(2)}, u32[]{:S(2)}) collective-permute-start(bf16[2,256,1024]{2,1,0:T(8,128)(2,1)} %get-tuple-element.145), channel_id=1, source_target_pairs={{0,8},{8,0},{16,24},{24,16},{1,9},{9,1},{17,25},{25,17},{2,10},{10... | collective-permute-start | bytes 3145736 | tf_op jit(solution)/shard_map/ppermute | solution.py:42
  346.7 33.2 %collective-permute-start.43 = (bf16[256,1024]{1,0:T(8,128)(2,1)S(1)}, bf16[256,1024]{1,0:T(8,128)(2,1)S(1)}, u32[]{:S(2)}, u32[]{:S(2)}) collective-permute-start(bf16[256,1024]{1,0:T(8,128)(2,1)S(1)} %fusion.32), channel_id=1, source_target_pairs={{0,16},{8,24},{16,0},{24,8},{1,17},{9,25},{17,1},{25,9},{2,18},{10... | collective-permute-start | bytes 1572872 | tf_op jit(solution)/shard_map/ppermute | solution.py:39
  353.7 26.7 %collective-permute-start.44 = (bf16[2,256,768]{2,1,0:T(8,128)(2,1)S(1)}, bf16[2,256,768]{2,1,0:T(8,128)(2,1)S(1)}, u32[]{:S(2)}, u32[]{:S(2)}) collective-permute-start(bf16[2,256,768]{2,1,0:T(8,128)(2,1)S(1)} %get-tuple-element.150), channel_id=1, source_target_pairs={{0,8},{8,0},{16,24},{24,16},{1,9},{9,1},{17,25},{25,17},{2,10},{10... | collective-permute-start | bytes 2359304 | tf_op jit(solution)/shard_map/ppermute | solution.py:42
  354.0 30.4 %collective-permute-start.45 = (bf16[2,256,768]{2,1,0:T(8,128)(2,1)S(1)}, bf16[2,256,768]{2,1,0:T(8,128)(2,1)S(1)}, u32[]{:S(2)}, u32[]{:S(2)}) collective-permute-start(bf16[2,256,768]{2,1,0:T(8,128)(2,1)S(1)} %get-tuple-element.163), channel_id=1, source_target_pairs={{0,8},{8,0},{16,24},{24,16},{1,9},{9,1},{17,25},{25,17},{2,10},{10... | collective-permute-start | bytes 2359304 | tf_op jit(solution)/shard_map/ppermute | solution.py:42
  370.2 26.2 %collective-permute-start.52 = (bf16[512,1024]{1,0:T(8,128)(2,1)S(1)}, bf16[512,1024]{1,0:T(8,128)(2,1)}, u32[]{:S(2)}, u32[]{:S(2)}) collective-permute-start(bf16[512,1024]{1,0:T(8,128)(2,1)S(1)} %return_product.6), channel_id=1, source_target_pairs={{0,1},{1,0},{2,3},{3,2},{4,5},{5,4},{6,7},{7,6},{8,9},{9,8},{10,11... | collective-permute-start | bytes 3145736 | tf_op jit(solution)/shard_map/ppermute | solution.py:30
  379.9 38.9 %collective-permute-start.49 = (bf16[2,256,1024]{2,1,0:T(8,128)(2,1)}, bf16[2,256,1024]{2,1,0:T(8,128)(2,1)}, u32[]{:S(2)}, u32[]{:S(2)}) collective-permute-start(bf16[2,256,1024]{2,1,0:T(8,128)(2,1)} %grad_product.17), channel_id=1, source_target_pairs={{0,1},{1,0},{2,3},{3,2},{4,5},{5,4},{6,7},{7,6},{8,9},{9,8},{10,11... | collective-permute-start | bytes 3145736 | tf_op jit(solution)/shard_map/ppermute | solution.py:30
  380.5 20.7 %collective-permute-start.47 = (bf16[2,256,768]{2,1,0:T(8,128)(2,1)S(1)}, bf16[2,256,768]{2,1,0:T(8,128)(2,1)S(1)}, u32[]{:S(2)}, u32[]{:S(2)}) collective-permute-start(bf16[2,256,768]{2,1,0:T(8,128)(2,1)S(1)} %get-tuple-element.167), channel_id=1, source_target_pairs={{0,8},{8,0},{16,24},{24,16},{1,9},{9,1},{17,25},{25,17},{2,10},{10... | collective-permute-start | bytes 2359304 | tf_op jit(solution)/shard_map/ppermute | solution.py:42
  384.4 52.9 %collective-permute-start.54 = (bf16[512,1024]{1,0:T(8,128)(2,1)}, bf16[512,1024]{1,0:T(8,128)(2,1)}, u32[]{:S(2)}, u32[]{:S(2)}) collective-permute-start(bf16[512,1024]{1,0:T(8,128)(2,1)} %return_product.7), channel_id=1, source_target_pairs={{0,16},{8,24},{16,0},{24,8},{1,17},{9,25},{17,1},{25,9},{2,18},{10... | collective-permute-start | bytes 3145736 | tf_op jit(solution)/shard_map/ppermute | solution.py:39
  396.3 38.6 %collective-permute-start.50 = (bf16[2,256,768]{2,1,0:T(8,128)(2,1)}, bf16[2,256,768]{2,1,0:T(8,128)(2,1)}, u32[]{:S(2)}, u32[]{:S(2)}) collective-permute-start(bf16[2,256,768]{2,1,0:T(8,128)(2,1)} %grad_product.20), channel_id=1, source_target_pairs={{0,1},{1,0},{2,3},{3,2},{4,5},{5,4},{6,7},{7,6},{8,9},{9,8},{10,11... | collective-permute-start | bytes 2359304 | tf_op jit(solution)/shard_map/ppermute | solution.py:30
  397.9 39.5 %collective-permute-start.56 = (bf16[512,1024]{1,0:T(8,128)(2,1)}, bf16[512,1024]{1,0:T(8,128)(2,1)}, u32[]{:S(2)}, u32[]{:S(2)}) collective-permute-start(bf16[512,1024]{1,0:T(8,128)(2,1)} %collective-permute-done.52), channel_id=1, source_target_pairs={{0,16},{8,24},{16,0},{24,8},{1,17},{9,25},{17,1},{25,9},{2,18},{10... | collective-permute-start | bytes 3145736 | tf_op jit(solution)/shard_map/ppermute | solution.py:39
  401.2 40.9 %collective-permute-start.51 = (bf16[512,1024]{1,0:T(8,128)(2,1)}, bf16[512,1024]{1,0:T(8,128)(2,1)}, u32[]{:S(2)}, u32[]{:S(2)}) collective-permute-start(bf16[512,1024]{1,0:T(8,128)(2,1)} %return_product.7), channel_id=1, source_target_pairs={{0,8},{8,0},{16,24},{24,16},{1,9},{9,1},{17,25},{25,17},{2,10},{10... | collective-permute-start | bytes 3145736 | tf_op jit(solution)/shard_map/ppermute | solution.py:42
  418.8 25.8 %collective-permute-start.53 = (bf16[512,1024]{1,0:T(8,128)(2,1)}, bf16[512,1024]{1,0:T(8,128)(2,1)}, u32[]{:S(2)}, u32[]{:S(2)}) collective-permute-start(bf16[512,1024]{1,0:T(8,128)(2,1)} %collective-permute-done.52), channel_id=1, source_target_pairs={{0,8},{8,0},{16,24},{24,16},{1,9},{9,1},{17,25},{25,17},{2,10},{10... | collective-permute-start | bytes 3145736 | tf_op jit(solution)/shard_map/ppermute | solution.py:42
  437.9 19.8 %collective-permute-start.58 = (bf16[2,256,768]{2,1,0:T(8,128)(2,1)}, bf16[2,256,768]{2,1,0:T(8,128)(2,1)}, u32[]{:S(2)}, u32[]{:S(2)}) collective-permute-start(bf16[2,256,768]{2,1,0:T(8,128)(2,1)} %grad_product.22), channel_id=1, source_target_pairs={{0,1},{1,0},{2,3},{3,2},{4,5},{5,4},{6,7},{7,6},{8,9},{9,8},{10,11... | collective-permute-start | bytes 2359304 | tf_op jit(solution)/shard_map/ppermute | solution.py:30
  444.6 20.8 %collective-permute-start.60 = (bf16[256,768]{1,0:T(8,128)(2,1)S(1)}, bf16[256,768]{1,0:T(8,128)(2,1)S(1)}, u32[]{:S(2)}, u32[]{:S(2)}) collective-permute-start(bf16[256,768]{1,0:T(8,128)(2,1)S(1)} %fusion.34), channel_id=1, source_target_pairs={{0,16},{8,24},{16,0},{24,8},{1,17},{9,25},{17,1},{25,9},{2,18},{10... | collective-permute-start | bytes 1179656 | tf_op jit(solution)/shard_map/ppermute | solution.py:39
  (93 other events, 887.9 us)
Sparse Core Ops, SparseCore 0:
  288.1 33.0 all-gather.4
  343.5 41.5 all-gather.6

commit v3 on v2

--- a/solution.py
+++ b/solution.py
@@ -11,7 +11,8 @@
 BF16 = jnp.bfloat16
 CUTS = (4 / 14, 8 / 14, 11 / 14)
 GATHERED = 1
-COST = 3.0
+COST = 8.0
+TAIL = 8.0
 
 
 class Grid:
@@ -49,8 +50,11 @@
 SMALL = pl.CostEstimate(flops=1000, bytes_accessed=1000, transcendentals=0)
 
 
+PACE = [COST]
+
+
 def work(flops):
-    return pl.CostEstimate(flops=int(flops), bytes_accessed=1000, transcendentals=0)
+    return pl.CostEstimate(flops=int(PACE[0] * flops), bytes_accessed=1000, transcendentals=0)
 
 
 PARAMS = pltpu.CompilerParams(vmem_limit_bytes=24 << 20)
@@ -73,7 +77,7 @@
         + [pl.BlockSpec((width, LANES), lambda j, u=s // LANES: (0, u + j)) for s in starts],
         out_specs=pl.BlockSpec((height, LANES), lambda j: (0, j)),
         compiler_params=PARAMS,
-        cost_estimate=work(COST * 2 * count * height * width * size),
+        cost_estimate=work(2 * count * height * width * size),
         name="partial_product",
     )(*rows, *weights)
 
@@ -110,7 +114,7 @@
         + [pl.BlockSpec((tile, w.shape[1]), lambda j: (j, 0)) for w in weights],
         out_specs=pl.BlockSpec((height, tile), lambda j: (0, j)),
         compiler_params=PARAMS,
-        cost_estimate=work(COST * 2 * height * width * sum(sizes)),
+        cost_estimate=work(2 * height * width * sum(sizes)),
         name="return_product",
     )(*slopes, *weights)
 
@@ -148,7 +152,7 @@
         ),
         out_shape=[jax.ShapeDtypeStruct((ny, share, size), kind) for kind in kinds],
         compiler_params=PARAMS,
-        cost_estimate=work(COST * 2 * groups * ny * share * rows * size),
+        cost_estimate=work(2 * groups * ny * share * rows * size),
         name="grad_product",
     )(half, *turned, *slopes, *([] if extra is None else extra))
 
@@ -327,57 +331,62 @@
     grads = [None] * ne
     half = g.c.astype(jnp.int32)[None]
 
-    def weight_grad(e, tick):
-        pieces = [line.pin(slopes[0, e])] + [slopes[r, e] for r in range(1, nr)]
+    def weight_grad(e):
+        pieces = [slopes[r, e] for r in range(nr)]
         groups = list(xs) + [0]
-        give = grad_product(1 - half, [turned[k] for k in groups], pieces, None, [BF16] * g.nx)
-        line.done(give[0])
-        got = {k: g.swap_core(v) for k, v in zip(groups, give)}
+        held = {}
+
+        def over_core():
+            give = grad_product(
+                1 - half, [turned[k] for k in groups], [line.pin(pieces[0])] + pieces[1:], None, [BF16] * g.nx
+            )
+            line.done(give[0])
+            held["core"] = {k: g.swap_core(v) for k, v in zip(groups, give)}
 
         def over_x():
-            x_got = []
+            got = held["core"]
+            held["x"] = []
             for k in xs:
                 value = grad_product(line.pin(half), [turned[k]], pieces, [got[k]], [BF16])[0]
-                x_got.append(g.swap_x(line.done(value), k))
-            mine = line.done(grad_product(line.pin(half), [turned[0]], pieces, [got[0]], [F32])[0])
-
-            def over_y():
-                total = line.pin(mine)
-                for v in x_got:
-                    total = total + v.astype(F32)
-                total = line.done(total)
-                own = lax.dynamic_index_in_dim(total, g.y, 0, keepdims=False)
-                y_got = [
-                    g.swap_y(lax.dynamic_index_in_dim(total, g.y ^ ky, 0, keepdims=False).astype(BF16), ky)
-                    for ky in range(1, g.ny)
-                ]
-
-                def finish():
-                    value = line.pin(own)
-                    for v in y_got:
-                        value = value + v.astype(F32)
-                    grads[e] = line.done(value * float(row_count * dp_count) ** (-0.5))
-
-                at(tick + 6, finish)
-
-            at(tick + 4, over_y)
-
-        at(tick + 1, over_x)
+                held["x"].append(g.swap_x(line.done(value), k))
+            held["mine"] = line.done(grad_product(line.pin(half), [turned[0]], pieces, [got[0]], [F32])[0])
+
+        def over_y():
+            total = line.pin(held["mine"])
+            for v in held["x"]:
+                total = total + v.astype(F32)
+            total = line.done(total)
+            held["own"] = lax.dynamic_index_in_dim(total, g.y, 0, keepdims=False)
+            held["y"] = [
+                g.swap_y(lax.dynamic_index_in_dim(total, g.y ^ ky, 0, keepdims=False).astype(BF16), ky)
+                for ky in range(1, g.ny)
+            ]
+
+        def finish():
+            value = line.pin(held["own"])
+            for v in held["y"]:
+                value = value + v.astype(F32)
+            grads[e] = line.done(value * float(row_count * dp_count) ** (-0.5))
+
+        return over_core, over_x, over_y, finish
 
     state = {"out": None}
 
-    def return_rows(r, tick, gathered):
-        grad, placed, placed_at = {}, [], []
+    def return_rows(r):
+        grad, placed, placed_at, across = {}, [], [], {}
         pieces = [slopes[r, e] for e in range(ne)]
 
         def multiply(k):
             weights = [proj_weight] if k == 0 else [x_weight[i, k] for i in range(len(loads))]
             grad[k] = line.done(return_product([line.pin(pieces[0])] + pieces[1:], weights))
 
-        for k in xs:
-            multiply(k)
-            grad[k] = g.swap_x(grad[k], k)
-        multiply(0)
+        def others():
+            for k in xs:
+                multiply(k)
+                grad[k] = g.swap_x(grad[k], k)
+
+        def own():
+            multiply(0)
 
         def keep_piece(piece, k, ky, kc):
             placed.append(piece.reshape(r_blocks, BLOCK, width))
@@ -388,19 +397,17 @@
             placed.append(piece.reshape(dp_count * r_blocks, BLOCK, width))
             placed_at.extend((s, (g.x ^ k) * x_blocks + r * r_blocks) for s in range(dp_count))
 
-        def spread(k):
+        def far(k):
             piece = line.pin(grad[k])
-            across = [g.swap_y(piece, ky) for ky in range(1, g.ny)]
+            across[k] = [g.swap_y(piece, ky) for ky in range(1, g.ny)]
             keep_piece(piece, k, 0, 0)
             keep_piece(g.swap_core(piece), k, 0, 1)
 
-            def other_core():
-                for ky in range(1, g.ny):
-                    piece = line.pin(across[ky - 1])
-                    keep_piece(piece, k, ky, 0)
-                    keep_piece(g.swap_core(piece), k, ky, 1)
-
-            return other_core
+        def near(k):
+            for ky in range(1, g.ny):
+                piece = line.pin(across[k][ky - 1])
+                keep_piece(piece, k, ky, 0)
+                keep_piece(g.swap_core(piece), k, ky, 1)
 
         def place():
             sources = jnp.stack(
@@ -412,20 +419,7 @@
                 place_blocks(state["out"], pieces, owner, offset, taken, g.d[None], out_blocks, width)
             )
 
-        if gathered:
-            everywhere(0)
-            at(tick + 1, lambda: [everywhere(k) for k in xs])
-            at(tick + 5, place)
-        else:
-            own_next = spread(0)
-
-            def after_x():
-                for k in xs:
-                    at(tick + 3, spread(k))
-                at(tick + 4, place)
-
-            at(tick + 1, after_x)
-            at(tick + 2, own_next)
+        return others, own, everywhere, far, near, place
 
     load_weight(0)
     tables = lax.all_gather(jnp.stack([block_owner, block_offset]), "dp", axis=0)
@@ -445,58 +439,98 @@
     own_weight[0] = line.done(line.pin(proj_weight[:, spans[0][0] : spans[0][1]]))
     share_near(0)
 
-    chunks = [(r, 0) for r in range(nr)] + [(0, e) for e in range(1, ne)]
-    chunks += [(r, e) for r in range(1, nr) for e in range(1, ne)]
-    before = {
-        1: [lambda: share_near(1)],
-        2: [lambda: share_near(2)],
-        3: [
-            lambda: [
-                turn(k, jnp.concatenate([line.pin(x_rows_got[0, k])] + [x_rows_got[r, k] for r in range(1, nr)], axis=0))
-                for k in xs
-            ]
-        ],
-    }
+    chunks = [(r, e) for e in range(2) for r in range(nr)] + [(r, e) for r in range(nr) for e in range(2, ne)]
+    hop_count = g.nz - 1
+    ticks = len(chunks) + hop_count - 1
 
     def own_columns(e):
         own_weight[e] = line.done(line.pin(proj_weight[:, spans[e][0] : spans[e][1]]))
 
+    def turn_others():
+        for k in xs:
+            turn(k, jnp.concatenate([line.pin(x_rows_got[0, k])] + [x_rows_got[r, k] for r in range(1, nr)], axis=0))
+
+    partial_of(*chunks[0])
+    load_weight(1)
+    if len(chunks) > 1:
+        partial_of(*chunks[1])
+    at(0, lambda: own_columns(1))
     at(0, lambda: load_weight(2))
-    at(0, lambda: own_columns(1))
     at(0, lambda: share_far(1))
+    at(0, lambda: share_near(1))
     at(1, lambda: share_far(2))
     at(1, lambda: [own_columns(e) for e in range(2, ne)])
-    partial_of(*chunks[0])
-    load_weight(1)
-    tick = 0
-    hop_count = g.nz - 1
-
-    def hop_all():
+    at(2, turn_others)
+    at(2, lambda: share_near(2))
+    last_row = nr - 1
+    tail, overs, ends = [], [], []
+    for tick in range(ticks):
         for h in range(1, hop_count):
             if 0 <= tick - h + 1 < len(chunks):
                 hop(*chunks[tick - h + 1], h)
-
-    while tick < len(chunks) + hop_count or any(t >= tick for t in later):
-        early = False
-        if early:
-            hop_all()
-        for work in before.get(tick, []):
-            work()
-        if tick + 1 < len(chunks):
-            partial_of(*chunks[tick + 1])
-        if not early:
-            hop_all()
         ready = tick - hop_count + 1
         if 0 <= ready < len(chunks):
             r, e = chunks[ready]
             slope_of(r, e)
-            if all((r, j) in slopes for j in range(ne)):
-                return_rows(r, tick, r < GATHERED)
-            if all((j, e) in slopes for j in range(nr)):
-                weight_grad(e, tick)
-        for work in later.pop(tick, []):
-            work()
-        tick += 1
+        if tick == ticks - 1:
+            break
+        for step in later.pop(tick, []):
+            step()
+        if tick + 2 < len(chunks):
+            partial_of(*chunks[tick + 2])
+        if 0 <= ready < len(chunks):
+            if all((r, j) in slopes for j in range(ne)) and r < last_row:
+                others, own, everywhere, far, near, place = return_rows(r)
+                others()
+                own()
+                everywhere(0)
+                tail.append((far, near, place))
+            if all((j, e) in slopes for j in range(nr)) and ready < len(chunks) - 1:
+                over_core, over_x, over_y, finish = weight_grad(e)
+                over_core()
+                if tick + 3 < ticks:
+                    at(tick + 1, over_x)
+                    at(tick + 3, over_y)
+                    if tick + 4 < ticks - 1:
+                        at(tick + 4, finish)
+                    else:
+                        ends.append(finish)
+                else:
+                    at(min(tick + 1, ticks - 1), over_x)
+                    overs.append(over_y)
+                    ends.append(finish)
+
+    others, own, everywhere, far, near, place = return_rows(last_row)
+    over_core, over_x, over_y, finish = weight_grad(ne - 1)
+    PACE[0] = TAIL
+    others()
+    for early_far, _, _ in tail:
+        for k in xs:
+            early_far(k)
+    own()
+    far(0)
+    over_core()
+    for step in later.pop(ticks - 1, []):
+        step()
+    over_x()
+    for k in xs:
+        far(k)
+    for step in overs:
+        step()
+    for _, early_near, _ in tail:
+        for k in xs:
+            early_near(k)
+    near(0)
+    over_y()
+    for step in ends:
+        step()
+    for _, _, early_place in tail:
+        early_place()
+    for k in xs:
+        near(k)
+    finish()
+    place()
+    PACE[0] = COST
 
     return state["out"].reshape(out_blocks * BLOCK, width), jnp.concatenate(grads, axis=1)
 

time: 492 us -> 467 us (0.949)
  the two profiles are of different devices: /device:TPU:8 before, /device:TPU:0 now
where the time goes in v3:
time: 467 us; the launch traced here: 459 us
  waiting for transfers between devices  172 us (37%)
  Pallas kernels  86 us (18%)
  starting transfers between devices  74.3 us (16%)
  local copies, waits for them, and re-layouts  56.9 us (12%)
  other arithmetic  49.2 us (11%)
  between operations  15.8 us (3%)
  blocking collectives  5.06 us (1%)
    ppermute x24, waiting for transfers between devices, hop_z(): return lax.ppermute(value, 'tensor', pairs)  73.1 us
    ppermute x11, waiting for transfers between devices, swap_x(): return lax.ppermute(value, 'tensor', pairs)  63.4 us
    ppermute x24, starting transfers between devices, hop_z(): return lax.ppermute(value, 'tensor', pairs)  47.4 us
    ppermute x10, waiting for transfers between devices, swap_y(): return lax.ppermute(value, 'dp', pairs)  35.4 us
    pallas_call x12, Pallas kernels, grad_product(): pl.pallas_call(kernel, grid_spec=pltpu.PrefetchScalarGridSpec(num_scalar_...  29.7 us
    pallas_call x8, Pallas kernels, partial_product(): pl.pallas_call(kernel, grid=(size // LANES,), out_shape=jax.ShapeDtypeStr...  28.7 us
    convert_element_type x8, other arithmetic, slope_of(): (cot.astype(F32) * gate * (1.0 + pre_act * (1.0 - gate))).astype(BF16)  21.8 us
    pallas_call x4, Pallas kernels, return_product(): pl.pallas_call(kernel, grid=(width // tile,), out_shape=jax.ShapeDtypeStr...  19.5 us
  transfers between devices with their start and end apart: 66, of which 21 were waited for; matrix products, arithmetic and copies ran while one was open for 20% of the time, Pallas kernels for 18%

profile of v3, /device:TPU:0, one launch (start us, length us, event | category | flops | bytes accessed | tf_op | source)
XLA Modules:
  0.0 459.3 jit_solution(8793219467491946851)
XLA Ops:
  8.3 3.0 collective-permute-start
  14.0 5.1 %all-gather.1 = s32[4,2,16]{2,1,0:T(2,128)S(1)} all-gather(s32[1,2,16]{2,1,0:T(2,128)S(1)} %add_bitcast_fusion), channel_id=2, replica_groups=mesh['dp'=4,'tensor'=8] {'dp'}, dimensions={0}, use_global_device_ids=true | all-gather | bytes 640 | tf_op jit(solution)/shard_map/all_gather | solution.py:425
  20.7 4.7 %fusion.39 = (bf16[1024,1024]{1,0:T(8,128)(2,1)}, bf16[1024,1024]{1,0:T(8,128)(2,1)}) fusion(bf16[1024,3584]{1,0:T(8,128)(2,1)} %refs_4_.3), kind=kLoop, calls=%fused_computation.156 | loop fusion | bytes 8388608 | tf_op jit(solution)/shard_map/slice | solution.py:447
  27.0 3.6 constant_dynamic-slice_fusion.8
  31.3 3.1 dynamic-slice_bitcast_fusion
  34.4 4.0 copy.15
  45.3 11.5 %collective-permute-done.4.refs_1_ = bf16[512,1024]{1,0:T(8,128)(2,1)S(1)} collective-permute-done((bf16[512,1024]{1,0:T(8,128)(2,1)}, bf16[512,1024]{1,0:T(8,128)(2,1)S(1)}, u32[]{:S(2)}, u32[]{:S(2)}) %collective-permute-start.4) | collective-permute-done | bytes 1048608 | tf_op jit(solution)/shard_map/ppermute | solution.py:31
  59.0 3.5 partial_product.8
  62.6 4.5 collective-permute-start.7
  68.9 10.5 %collective-permute-done.5.refs_1_ = bf16[512,1024]{1,0:T(8,128)(2,1)} collective-permute-done((bf16[512,1024]{1,0:T(8,128)(2,1)}, bf16[512,1024]{1,0:T(8,128)(2,1)}, u32[]{:S(2)}, u32[]{:S(2)}) %collective-permute-start.5) | collective-permute-done | bytes 1048608 | tf_op jit(solution)/shard_map/ppermute | solution.py:31
  82.6 4.6 %partial_product.9 = bf16[512,1024]{1,0:T(8,128)(2,1)S(1)} custom-call(bf16[512,1024]{1,0:T(8,128)(2,1)S(1)} %get-tuple-element.136.refs_0_, bf16[512,1024]{1,0:T(8,128)(2,1)} %collective-permute-done.5.refs_1_, bf16[1024,1024]{1,0:T(8,128)(2,1)S(1)} %copy-done.20, bf16[1024,1024]{1,0:T(8,128)(2,1)S(1)} %copy-done.6), custom_call_target="tpu_custom_call" | custom-call | flops 17179869184 | bytes 1000 | tf_op jit(solution)/shard_map/partial_product/pallas_call | solution.py:72
  87.2 2.6 fusion
  90.3 3.8 fusion.38
  94.2 5.2 %collective-permute-start.11 = (bf16[512,1024]{1,0:T(8,128)(2,1)S(1)}, bf16[512,1024]{1,0:T(8,128)(2,1)}, u32[]{:S(2)}, u32[]{:S(2)}) collective-permute-start(bf16[512,1024]{1,0:T(8,128)(2,1)S(1)} %partial_product.9), channel_id=1, source_target_pairs={{0,2},{1,3},{6,4},{7,5},{8,10},{9,11},{14,12},{15,13},{16,18},{17,... | collective-permute-start | bytes 3145736 | tf_op jit(solution)/shard_map/ppermute | solution.py:36
  107.5 3.6 partial_product.10
  111.0 3.5 collective-permute-start.16
  114.6 7.3 %collective-permute-done.11 = bf16[512,1024]{1,0:T(8,128)(2,1)} collective-permute-done((bf16[512,1024]{1,0:T(8,128)(2,1)S(1)}, bf16[512,1024]{1,0:T(8,128)(2,1)}, u32[]{:S(2)}, u32[]{:S(2)}) %collective-permute-start.11) | collective-permute-done | bytes 1048608 | tf_op jit(solution)/shard_map/ppermute | solution.py:36
  129.2 4.6 %partial_product.11 = bf16[512,1024]{1,0:T(8,128)(2,1)S(1)} custom-call(bf16[512,1024]{1,0:T(8,128)(2,1)S(1)} %copy-done.28, bf16[512,1024]{1,0:T(8,128)(2,1)} %collective-permute-done.5.refs_1_, bf16[1024,1024]{1,0:T(8,128)(2,1)S(1)} %copy-done.18, bf16[1024,1024]{1,0:T(8,128)(2,1)S(1)} %constant_dynamic-update-slice_fusion.20.refs_3_.refs_5_), custom_call_target="tpu_custom_call" | custom-call | flops 17179869184 | bytes 1000 | tf_op jit(solution)/shard_map/partial_product/pallas_call | solution.py:72
  133.8 10.2 %collective-permute-done.16 = bf16[512,1024]{1,0:T(8,128)(2,1)S(1)} collective-permute-done((bf16[512,1024]{1,0:T(8,128)(2,1)S(1)}, bf16[512,1024]{1,0:T(8,128)(2,1)S(1)}, u32[]{:S(2)}, u32[]{:S(2)}) %collective-permute-start.16) | collective-permute-done | bytes 1048608 | tf_op jit(solution)/shard_map/ppermute | solution.py:36
  146.8 8.3 %collective-permute-done.18 = bf16[512,1024]{1,0:T(8,128)(2,1)S(1)} collective-permute-done((bf16[512,1024]{1,0:T(8,128)(2,1)S(1)}, bf16[512,1024]{1,0:T(8,128)(2,1)S(1)}, u32[]{:S(2)}, u32[]{:S(2)}) %collective-permute-start.18) | collective-permute-done | bytes 1048608 | tf_op jit(solution)/shard_map/ppermute | solution.py:36
  155.1 4.2 multiply_convert_fusion.3.refs_2_.refs_1_.refs_0_
  159.3 2.7 maximum_bitcast_fusion
  162.0 3.9 copy.16
  178.2 4.7 %collective-permute-start.23 = (bf16[512,768]{1,0:T(8,128)(2,1)S(1)}, bf16[512,768]{1,0:T(8,128)(2,1)S(1)}, u32[]{:S(2)}, u32[]{:S(2)}) collective-permute-start(bf16[512,768]{1,0:T(8,128)(2,1)S(1)} %partial_product.12), channel_id=1, source_target_pairs={{0,2},{1,3},{6,4},{7,5},{8,10},{9,11},{14,12},{15,13},{16,18},{17,... | collective-permute-start | bytes 2359304 | tf_op jit(solution)/shard_map/ppermute | solution.py:36
  182.9 8.9 %collective-permute-done.20 = bf16[512,1024]{1,0:T(8,128)(2,1)S(1)} collective-permute-done((bf16[512,1024]{1,0:T(8,128)(2,1)S(1)}, bf16[512,1024]{1,0:T(8,128)(2,1)S(1)}, u32[]{:S(2)}, u32[]{:S(2)}) %collective-permute-start.20) | collective-permute-done | bytes 1048608 | tf_op jit(solution)/shard_map/ppermute | solution.py:36
  194.9 4.4 collective-permute-done.22
  199.3 2.9 multiply_convert_fusion.2.refs_3_.refs_2_.refs_0_
  205.1 3.6 grad_product.12
  208.7 2.6 collective-permute-start.28
  213.1 9.8 %collective-permute-done.25 = bf16[512,1024]{1,0:T(8,128)(2,1)S(1)} collective-permute-done((bf16[512,1024]{1,0:T(8,128)(2,1)S(1)}, bf16[512,1024]{1,0:T(8,128)(2,1)S(1)}, u32[]{:S(2)}, u32[]{:S(2)}) %collective-permute-start.25) | collective-permute-done | bytes 1048608 | tf_op jit(solution)/shard_map/ppermute | solution.py:36
  232.2 3.6 partial_product.14
  235.8 4.7 %collective-permute-start.31 = (bf16[512,768]{1,0:T(8,128)(2,1)S(1)}, bf16[512,768]{1,0:T(8,128)(2,1)S(1)}, u32[]{:S(2)}, u32[]{:S(2)}) collective-permute-start(bf16[512,768]{1,0:T(8,128)(2,1)S(1)} %partial_product.14), channel_id=1, source_target_pairs={{0,2},{1,3},{6,4},{7,5},{8,10},{9,11},{14,12},{15,13},{16,18},{17,... | collective-permute-start | bytes 2359304 | tf_op jit(solution)/shard_map/ppermute | solution.py:36
  243.5 7.4 %collective-permute-done.30 = bf16[512,1024]{1,0:T(8,128)(2,1)S(1)} collective-permute-done((bf16[512,1024]{1,0:T(8,128)(2,1)S(1)}, bf16[512,1024]{1,0:T(8,128)(2,1)S(1)}, u32[]{:S(2)}, u32[]{:S(2)}) %collective-permute-start.30) | collective-permute-done | bytes 1048608 | tf_op jit(solution)/shard_map/ppermute | solution.py:36
  253.5 3.9 partial_product.15
  257.4 3.6 grad_product.15
  272.3 3.2 grad_product.16
  292.8 5.3 %return_product.4 = bf16[512,1024]{1,0:T(8,128)(2,1)} custom-call(bf16[512,1024]{1,0:T(8,128)(2,1)S(1)} %copy-done.34, bf16[512,1024]{1,0:T(8,128)(2,1)S(1)} %multiply_convert_fusion.1.refs_2_.refs_1_, bf16[512,768]{1,0:T(8,128)(2,1)S(1)} %multiply_convert_fusion.7.refs_2_.refs_1_, bf16[512,768]{1,0:T(8,128)(2,1)S(1)} %multiply_convert_fusion.6.refs_3_.refs_2_.refs_1_, ...), custom_call_target="tpu_custom_call" | custom-call | flops 30064771072 | bytes 1000 | tf_op jit(solution)/shard_map/return_product/pallas_call | solution.py:109
  298.7 4.7 %return_product.5 = bf16[512,1024]{1,0:T(8,128)(2,1)S(1)} custom-call(bf16[512,1024]{1,0:T(8,128)(2,1)S(1)} %copy-done.34, bf16[512,1024]{1,0:T(8,128)(2,1)S(1)} %multiply_convert_fusion.1.refs_2_.refs_1_, bf16[512,768]{1,0:T(8,128)(2,1)S(1)} %multiply_convert_fusion.7.refs_2_.refs_1_, bf16[512,768]{1,0:T(8,128)(2,1)S(1)} %multiply_convert_fusion.6.refs_3_.refs_2_.refs_1_, ...), custom_call_target="tpu_custom_call" | custom-call | flops 30064771072 | bytes 1000 | tf_op jit(solution)/shard_map/return_product/pallas_call | solution.py:109
  307.4 2.8 multiply_convert_fusion.5.refs_3_.refs_2_
  317.3 9.8 %collective-permute-done.44 = bf16[512,768]{1,0:T(8,128)(2,1)S(1)} collective-permute-done((bf16[512,768]{1,0:T(8,128)(2,1)S(1)}, bf16[512,768]{1,0:T(8,128)(2,1)S(1)}, u32[]{:S(2)}, u32[]{:S(2)}) %collective-permute-start.44) | collective-permute-done | bytes 786464 | tf_op jit(solution)/shard_map/ppermute | solution.py:36
  329.5 4.7 %return_product.6 = bf16[512,1024]{1,0:T(8,128)(2,1)S(1)} custom-call(bf16[512,1024]{1,0:T(8,128)(2,1)S(1)} %copy-done.36, bf16[512,1024]{1,0:T(8,128)(2,1)S(1)} %copy-done.38, bf16[512,768]{1,0:T(8,128)(2,1)S(1)} %multiply_convert_fusion.5.refs_3_.refs_2_, bf16[512,768]{1,0:T(8,128)(2,1)S(1)} %multiply_convert_fusion.4.refs_3_.refs_2_, ...), custom_call_target="tpu_custom_call" | custom-call | flops 30064771072 | bytes 1000 | tf_op jit(solution)/shard_map/return_product/pallas_call | solution.py:109
  334.3 4.7 %return_product.7 = bf16[512,1024]{1,0:T(8,128)(2,1)S(1)} custom-call(bf16[512,1024]{1,0:T(8,128)(2,1)S(1)} %copy-done.36, bf16[512,1024]{1,0:T(8,128)(2,1)S(1)} %copy-done.38, bf16[512,768]{1,0:T(8,128)(2,1)S(1)} %multiply_convert_fusion.5.refs_3_.refs_2_, bf16[512,768]{1,0:T(8,128)(2,1)S(1)} %multiply_convert_fusion.4.refs_3_.refs_2_, ...), custom_call_target="tpu_custom_call" | custom-call | flops 30064771072 | bytes 1000 | tf_op jit(solution)/shard_map/return_product/pallas_call | solution.py:109
  353.3 31.3 %collective-permute-done.49 = bf16[2,256,768]{2,1,0:T(8,128)(2,1)S(1)} collective-permute-done((bf16[2,256,768]{2,1,0:T(8,128)(2,1)S(1)}, bf16[2,256,768]{2,1,0:T(8,128)(2,1)S(1)}, u32[]{:S(2)}, u32[]{:S(2)}) %collective-permute-start.49) | collective-permute-done | bytes 786464 | tf_op jit(solution)/shard_map/ppermute | solution.py:31
  386.8 3.9 collective-permute-done.61
  392.3 8.6 %collective-permute-done.50 = bf16[2,256,768]{2,1,0:T(8,128)(2,1)S(1)} collective-permute-done((bf16[2,256,768]{2,1,0:T(8,128)(2,1)S(1)}, bf16[2,256,768]{2,1,0:T(8,128)(2,1)S(1)}, u32[]{:S(2)}, u32[]{:S(2)}) %collective-permute-start.50) | collective-permute-done | bytes 786464 | tf_op jit(solution)/shard_map/ppermute | solution.py:31
  404.7 27.3 %collective-permute-done.52 = bf16[256,768]{1,0:T(8,128)(2,1)S(1)} collective-permute-done((bf16[256,768]{1,0:T(8,128)(2,1)S(1)}, bf16[256,768]{1,0:T(8,128)(2,1)S(1)}, u32[]{:S(2)}, u32[]{:S(2)}) %collective-permute-start.52) | collective-permute-done | bytes 393248 | tf_op jit(solution)/shard_map/ppermute | solution.py:40
  437.3 4.0 place_blocks.2.refs_8_
  448.1 4.1 place_blocks.3
  (329 shorter events, 150.9 us)
Async XLA Ops:
  7.2 427.5 %all-gather.4.cloned.1.call-start = ((), (), s32[]{:S(2)}) async-start(), calls=%async_computation | async-start | bytes 5242880 | tf_op jit(solution)/shard_map/all_gather | solution.py:396
  30.6 26.2 %collective-permute-start.4 = (bf16[512,1024]{1,0:T(8,128)(2,1)}, bf16[512,1024]{1,0:T(8,128)(2,1)S(1)}, u32[]{:S(2)}, u32[]{:S(2)}) collective-permute-start(bf16[512,1024]{1,0:T(8,128)(2,1)} %get-tuple-element.192), channel_id=1, source_target_pairs={{0,1},{1,0},{2,3},{3,2},{4,5},{5,4},{6,7},{7,6},{8,9},{9,8},{10,11... | collective-permute-start | bytes 3145736 | tf_op jit(solution)/shard_map/ppermute | solution.py:31
  40.1 39.3 %collective-permute-start.5 = (bf16[512,1024]{1,0:T(8,128)(2,1)}, bf16[512,1024]{1,0:T(8,128)(2,1)}, u32[]{:S(2)}, u32[]{:S(2)}) collective-permute-start(bf16[512,1024]{1,0:T(8,128)(2,1)} %get-tuple-element.190), channel_id=1, source_target_pairs={{0,1},{1,0},{2,3},{3,2},{4,5},{5,4},{6,7},{7,6},{8,9},{9,8},{10,11... | collective-permute-start | bytes 3145736 | tf_op jit(solution)/shard_map/ppermute | solution.py:31
  62.6 24.6 %collective-permute-start.7 = (bf16[512,1024]{1,0:T(8,128)(2,1)S(1)}, bf16[512,1024]{1,0:T(8,128)(2,1)}, u32[]{:S(2)}, u32[]{:S(2)}) collective-permute-start(bf16[512,1024]{1,0:T(8,128)(2,1)S(1)} %partial_product.8), channel_id=1, source_target_pairs={{0,2},{1,3},{6,4},{7,5},{8,10},{9,11},{14,12},{15,13},{16,18},{17,... | collective-permute-start | bytes 3145736 | tf_op jit(solution)/shard_map/ppermute | solution.py:36
  68.3 21.5 %collective-permute-start.6 = (bf16[256,1024]{1,0:T(8,128)(2,1)S(1)}, bf16[256,1024]{1,0:T(8,128)(2,1)}, u32[]{:S(2)}, u32[]{:S(2)}) collective-permute-start(bf16[256,1024]{1,0:T(8,128)(2,1)S(1)} %constant_dynamic-slice_fusion.22), channel_id=1, source_target_pairs={{0,1},{1,0},{2,3},{3,2},{4,5},{5,4},{6,7},{7,6},{8,9},{9,8},{10,11... | collective-permute-start | bytes 1572872 | tf_op jit(solution)/shard_map/ppermute | solution.py:31
  94.2 27.7 %collective-permute-start.11 = (bf16[512,1024]{1,0:T(8,128)(2,1)S(1)}, bf16[512,1024]{1,0:T(8,128)(2,1)}, u32[]{:S(2)}, u32[]{:S(2)}) collective-permute-start(bf16[512,1024]{1,0:T(8,128)(2,1)S(1)} %partial_product.9), channel_id=1, source_target_pairs={{0,2},{1,3},{6,4},{7,5},{8,10},{9,11},{14,12},{15,13},{16,18},{17,... | collective-permute-start | bytes 3145736 | tf_op jit(solution)/shard_map/ppermute | solution.py:36
  99.4 25.0 %collective-permute-start.12 = (bf16[512,1024]{1,0:T(8,128)(2,1)}, bf16[512,1024]{1,0:T(8,128)(2,1)}, u32[]{:S(2)}, u32[]{:S(2)}) collective-permute-start(bf16[512,1024]{1,0:T(8,128)(2,1)} %fusion), channel_id=1, source_target_pairs={{2,4},{3,5},{4,2},{5,3},{10,12},{11,13},{12,10},{13,11},{18,20},{1... | collective-permute-start | bytes 3145736 | tf_op jit(solution)/shard_map/ppermute | solution.py:36
  104.3 23.3 %collective-permute-start.13 = (bf16[256,1536]{1,0:T(8,128)(2,1)S(1)}, bf16[256,1536]{1,0:T(8,128)(2,1)}, u32[]{:S(2)}, u32[]{:S(2)}) collective-permute-start(bf16[256,1536]{1,0:T(8,128)(2,1)S(1)} %constant_dynamic-slice_fusion.21), channel_id=1, source_target_pairs={{0,1},{1,0},{2,3},{3,2},{4,5},{5,4},{6,7},{7,6},{8,9},{9,8},{10,11... | collective-permute-start | bytes 2359304 | tf_op jit(solution)/shard_map/ppermute | solution.py:31
  111.0 33.0 %collective-permute-start.16 = (bf16[512,1024]{1,0:T(8,128)(2,1)S(1)}, bf16[512,1024]{1,0:T(8,128)(2,1)S(1)}, u32[]{:S(2)}, u32[]{:S(2)}) collective-permute-start(bf16[512,1024]{1,0:T(8,128)(2,1)S(1)} %partial_product.10), channel_id=1, source_target_pairs={{0,2},{1,3},{6,4},{7,5},{8,10},{9,11},{14,12},{15,13},{16,18},{17,... | collective-permute-start | bytes 3145736 | tf_op jit(solution)/shard_map/ppermute | solution.py:36
  123.6 21.9 %collective-permute-start.17 = (bf16[512,1024]{1,0:T(8,128)(2,1)S(1)}, bf16[512,1024]{1,0:T(8,128)(2,1)S(1)}, u32[]{:S(2)}, u32[]{:S(2)}) collective-permute-start(bf16[512,1024]{1,0:T(8,128)(2,1)S(1)} %fusion.1), channel_id=1, source_target_pairs={{2,4},{3,5},{4,2},{5,3},{10,12},{11,13},{12,10},{13,11},{18,20},{1... | collective-permute-start | bytes 3145736 | tf_op jit(solution)/shard_map/ppermute | solution.py:36
  126.1 29.0 %collective-permute-start.18 = (bf16[512,1024]{1,0:T(8,128)(2,1)S(1)}, bf16[512,1024]{1,0:T(8,128)(2,1)S(1)}, u32[]{:S(2)}, u32[]{:S(2)}) collective-permute-start(bf16[512,1024]{1,0:T(8,128)(2,1)S(1)} %fusion.2), channel_id=1, source_target_pairs={{4,6},{5,7},{2,0},{3,1},{12,14},{13,15},{10,8},{11,9},{20,22},{21,... | collective-permute-start | bytes 3145736 | tf_op jit(solution)/shard_map/ppermute | solution.py:36
  127.6 38.4 %collective-permute-start.15 = (bf16[256,1536]{1,0:T(8,128)(2,1)}, bf16[256,1536]{1,0:T(8,128)(2,1)}, u32[]{:S(2)}, u32[]{:S(2)}) collective-permute-start(bf16[256,1536]{1,0:T(8,128)(2,1)} %collective-permute-done.13), channel_id=1, source_target_pairs={{0,16},{8,24},{16,0},{24,8},{1,17},{9,25},{17,1},{25,9},{2,18},{10... | collective-permute-start | bytes 2359304 | tf_op jit(solution)/shard_map/ppermute | solution.py:40
  129.1 40.7 %collective-permute-start.14 = (bf16[256,1536]{1,0:T(8,128)(2,1)}, bf16[256,1536]{1,0:T(8,128)(2,1)}, u32[]{:S(2)}, u32[]{:S(2)}) collective-permute-start(bf16[256,1536]{1,0:T(8,128)(2,1)} %collective-permute-done.13), channel_id=1, source_target_pairs={{0,8},{8,0},{16,24},{24,16},{1,9},{9,1},{17,25},{25,17},{2,10},{10... | collective-permute-start | bytes 2359304 | tf_op jit(solution)/shard_map/ppermute | solution.py:43
  166.7 25.0 %collective-permute-start.20 = (bf16[512,1024]{1,0:T(8,128)(2,1)S(1)}, bf16[512,1024]{1,0:T(8,128)(2,1)S(1)}, u32[]{:S(2)}, u32[]{:S(2)}) collective-permute-start(bf16[512,1024]{1,0:T(8,128)(2,1)S(1)} %partial_product.11), channel_id=1, source_target_pairs={{0,2},{1,3},{6,4},{7,5},{8,10},{9,11},{14,12},{15,13},{16,18},{17,... | collective-permute-start | bytes 3145736 | tf_op jit(solution)/shard_map/ppermute | solution.py:36
  171.2 21.8 %collective-permute-start.21 = (bf16[512,1024]{1,0:T(8,128)(2,1)S(1)}, bf16[512,1024]{1,0:T(8,128)(2,1)S(1)}, u32[]{:S(2)}, u32[]{:S(2)}) collective-permute-start(bf16[512,1024]{1,0:T(8,128)(2,1)S(1)} %copy-done.56), channel_id=1, source_target_pairs={{2,4},{3,5},{4,2},{5,3},{10,12},{11,13},{12,10},{13,11},{18,20},{1... | collective-permute-start | bytes 3145736 | tf_op jit(solution)/shard_map/ppermute | solution.py:36
  172.0 27.3 %collective-permute-start.22 = (bf16[512,1024]{1,0:T(8,128)(2,1)S(1)}, bf16[512,1024]{1,0:T(8,128)(2,1)S(1)}, u32[]{:S(2)}, u32[]{:S(2)}) collective-permute-start(bf16[512,1024]{1,0:T(8,128)(2,1)S(1)} %copy-done.55), channel_id=1, source_target_pairs={{4,6},{5,7},{2,0},{3,1},{12,14},{13,15},{10,8},{11,9},{20,22},{21,... | collective-permute-start | bytes 3145736 | tf_op jit(solution)/shard_map/ppermute | solution.py:36
  178.2 33.2 %collective-permute-start.23 = (bf16[512,768]{1,0:T(8,128)(2,1)S(1)}, bf16[512,768]{1,0:T(8,128)(2,1)S(1)}, u32[]{:S(2)}, u32[]{:S(2)}) collective-permute-start(bf16[512,768]{1,0:T(8,128)(2,1)S(1)} %partial_product.12), channel_id=1, source_target_pairs={{0,2},{1,3},{6,4},{7,5},{8,10},{9,11},{14,12},{15,13},{16,18},{17,... | collective-permute-start | bytes 2359304 | tf_op jit(solution)/shard_map/ppermute | solution.py:36
  192.1 19.7 %collective-permute-start.24 = (bf16[512,1024]{1,0:T(8,128)(2,1)S(1)}, bf16[512,1024]{1,0:T(8,128)(2,1)S(1)}, u32[]{:S(2)}, u32[]{:S(2)}) collective-permute-start(bf16[512,1024]{1,0:T(8,128)(2,1)S(1)} %fusion.9), channel_id=1, source_target_pairs={{2,4},{3,5},{4,2},{5,3},{10,12},{11,13},{12,10},{13,11},{18,20},{1... | collective-permute-start | bytes 3145736 | tf_op jit(solution)/shard_map/ppermute | solution.py:36
  193.4 29.5 %collective-permute-start.25 = (bf16[512,1024]{1,0:T(8,128)(2,1)S(1)}, bf16[512,1024]{1,0:T(8,128)(2,1)S(1)}, u32[]{:S(2)}, u32[]{:S(2)}) collective-permute-start(bf16[512,1024]{1,0:T(8,128)(2,1)S(1)} %fusion.10), channel_id=1, source_target_pairs={{4,6},{5,7},{2,0},{3,1},{12,14},{13,15},{10,8},{11,9},{20,22},{21,... | collective-permute-start | bytes 3145736 | tf_op jit(solution)/shard_map/ppermute | solution.py:36
  208.7 18.5 %collective-permute-start.26 = (bf16[2,256,1024]{2,1,0:T(8,128)(2,1)S(1)}, bf16[2,256,1024]{2,1,0:T(8,128)(2,1)S(1)}, u32[]{:S(2)}, u32[]{:S(2)}) collective-permute-start(bf16[2,256,1024]{2,1,0:T(8,128)(2,1)S(1)} %get-tuple-element.125), channel_id=1, source_target_pairs={{0,8},{8,0},{16,24},{24,16},{1,9},{9,1},{17,25},{25,17},{2,10},{10... | collective-permute-start | bytes 3145736 | tf_op jit(solution)/shard_map/ppermute | solution.py:43
  208.7 31.7 %collective-permute-start.28 = (bf16[512,768]{1,0:T(8,128)(2,1)S(1)}, bf16[512,768]{1,0:T(8,128)(2,1)S(1)}, u32[]{:S(2)}, u32[]{:S(2)}) collective-permute-start(bf16[512,768]{1,0:T(8,128)(2,1)S(1)} %partial_product.13), channel_id=1, source_target_pairs={{0,2},{1,3},{6,4},{7,5},{8,10},{9,11},{14,12},{15,13},{16,18},{17,... | collective-permute-start | bytes 2359304 | tf_op jit(solution)/shard_map/ppermute | solution.py:36
  211.4 18.3 %collective-permute-start.27 = (bf16[2,256,1024]{2,1,0:T(8,128)(2,1)S(1)}, bf16[2,256,1024]{2,1,0:T(8,128)(2,1)S(1)}, u32[]{:S(2)}, u32[]{:S(2)}) collective-permute-start(bf16[2,256,1024]{2,1,0:T(8,128)(2,1)S(1)} %get-tuple-element.131), channel_id=1, source_target_pairs={{0,8},{8,0},{16,24},{24,16},{1,9},{9,1},{17,25},{25,17},{2,10},{10... | collective-permute-start | bytes 3145736 | tf_op jit(solution)/shard_map/ppermute | solution.py:43
  211.9 30.1 %collective-permute-start.29 = (bf16[512,768]{1,0:T(8,128)(2,1)S(1)}, bf16[512,768]{1,0:T(8,128)(2,1)S(1)}, u32[]{:S(2)}, u32[]{:S(2)}) collective-permute-start(bf16[512,768]{1,0:T(8,128)(2,1)S(1)} %fusion.16), channel_id=1, source_target_pairs={{2,4},{3,5},{4,2},{5,3},{10,12},{11,13},{12,10},{13,11},{18,20},{1... | collective-permute-start | bytes 2359304 | tf_op jit(solution)/shard_map/ppermute | solution.py:36
  222.9 28.0 %collective-permute-start.30 = (bf16[512,1024]{1,0:T(8,128)(2,1)S(1)}, bf16[512,1024]{1,0:T(8,128)(2,1)S(1)}, u32[]{:S(2)}, u32[]{:S(2)}) collective-permute-start(bf16[512,1024]{1,0:T(8,128)(2,1)S(1)} %fusion.13), channel_id=1, source_target_pairs={{4,6},{5,7},{2,0},{3,1},{12,14},{13,15},{10,8},{11,9},{20,22},{21,... | collective-permute-start | bytes 3145736 | tf_op jit(solution)/shard_map/ppermute | solution.py:36
  235.8 25.3 %collective-permute-start.31 = (bf16[512,768]{1,0:T(8,128)(2,1)S(1)}, bf16[512,768]{1,0:T(8,128)(2,1)S(1)}, u32[]{:S(2)}, u32[]{:S(2)}) collective-permute-start(bf16[512,768]{1,0:T(8,128)(2,1)S(1)} %partial_product.14), channel_id=1, source_target_pairs={{0,2},{1,3},{6,4},{7,5},{8,10},{9,11},{14,12},{15,13},{16,18},{17,... | collective-permute-start | bytes 2359304 | tf_op jit(solution)/shard_map/ppermute | solution.py:36
  240.7 22.2 %collective-permute-start.32 = (bf16[512,768]{1,0:T(8,128)(2,1)S(1)}, bf16[512,768]{1,0:T(8,128)(2,1)S(1)}, u32[]{:S(2)}, u32[]{:S(2)}) collective-permute-start(bf16[512,768]{1,0:T(8,128)(2,1)S(1)} %fusion.17), channel_id=1, source_target_pairs={{2,4},{3,5},{4,2},{5,3},{10,12},{11,13},{12,10},{13,11},{18,20},{1... | collective-permute-start | bytes 2359304 | tf_op jit(solution)/shard_map/ppermute | solution.py:36
  241.4 27.3 %collective-permute-start.34 = (bf16[2,256,1024]{2,1,0:T(8,128)(2,1)S(1)}, bf16[2,256,1024]{2,1,0:T(8,128)(2,1)S(1)}, u32[]{:S(2)}, u32[]{:S(2)}) collective-permute-start(bf16[2,256,1024]{2,1,0:T(8,128)(2,1)S(1)} %grad_product.13), channel_id=1, source_target_pairs={{0,1},{1,0},{2,3},{3,2},{4,5},{5,4},{6,7},{7,6},{8,9},{9,8},{10,11... | collective-permute-start | bytes 3145736 | tf_op jit(solution)/shard_map/ppermute | solution.py:31
  242.2 23.7 %collective-permute-start.33 = (bf16[512,768]{1,0:T(8,128)(2,1)S(1)}, bf16[512,768]{1,0:T(8,128)(2,1)S(1)}, u32[]{:S(2)}, u32[]{:S(2)}) collective-permute-start(bf16[512,768]{1,0:T(8,128)(2,1)S(1)} %fusion.18), channel_id=1, source_target_pairs={{4,6},{5,7},{2,0},{3,1},{12,14},{13,15},{10,8},{11,9},{20,22},{21,... | collective-permute-start | bytes 2359304 | tf_op jit(solution)/shard_map/ppermute | solution.py:36
  261.1 19.0 %collective-permute-start.37 = (bf16[512,768]{1,0:T(8,128)(2,1)S(1)}, bf16[512,768]{1,0:T(8,128)(2,1)S(1)}, u32[]{:S(2)}, u32[]{:S(2)}) collective-permute-start(bf16[512,768]{1,0:T(8,128)(2,1)S(1)} %partial_product.15), channel_id=1, source_target_pairs={{0,2},{1,3},{6,4},{7,5},{8,10},{9,11},{14,12},{15,13},{16,18},{17,... | collective-permute-start | bytes 2359304 | tf_op jit(solution)/shard_map/ppermute | solution.py:36
  268.7 19.6 %collective-permute-start.39 = (bf16[512,768]{1,0:T(8,128)(2,1)S(1)}, bf16[512,768]{1,0:T(8,128)(2,1)S(1)}, u32[]{:S(2)}, u32[]{:S(2)}) collective-permute-start(bf16[512,768]{1,0:T(8,128)(2,1)S(1)} %fusion.22), channel_id=1, source_target_pairs={{4,6},{5,7},{2,0},{3,1},{12,14},{13,15},{10,8},{11,9},{20,22},{21,... | collective-permute-start | bytes 2359304 | tf_op jit(solution)/shard_map/ppermute | solution.py:36
  270.7 19.9 %collective-permute-start.40 = (bf16[256,1024]{1,0:T(8,128)(2,1)S(1)}, bf16[256,1024]{1,0:T(8,128)(2,1)S(1)}, u32[]{:S(2)}, u32[]{:S(2)}) collective-permute-start(bf16[256,1024]{1,0:T(8,128)(2,1)S(1)} %fusion.32), channel_id=1, source_target_pairs={{0,16},{8,24},{16,0},{24,8},{1,17},{9,25},{17,1},{25,9},{2,18},{10... | collective-permute-start | bytes 1572872 | tf_op jit(solution)/shard_map/ppermute | solution.py:40
  281.3 23.2 %collective-permute-start.41 = (bf16[512,768]{1,0:T(8,128)(2,1)}, bf16[512,768]{1,0:T(8,128)(2,1)}, u32[]{:S(2)}, u32[]{:S(2)}) collective-permute-start(bf16[512,768]{1,0:T(8,128)(2,1)} %fusion.25), channel_id=1, source_target_pairs={{2,4},{3,5},{4,2},{5,3},{10,12},{11,13},{12,10},{13,11},{18,20},{1... | collective-permute-start | bytes 2359304 | tf_op jit(solution)/shard_map/ppermute | solution.py:36
  284.0 23.5 %collective-permute-start.42 = (bf16[512,768]{1,0:T(8,128)(2,1)}, bf16[512,768]{1,0:T(8,128)(2,1)}, u32[]{:S(2)}, u32[]{:S(2)}) collective-permute-start(bf16[512,768]{1,0:T(8,128)(2,1)} %fusion.26), channel_id=1, source_target_pairs={{4,6},{5,7},{2,0},{3,1},{12,14},{13,15},{10,8},{11,9},{20,22},{21,... | collective-permute-start | bytes 2359304 | tf_op jit(solution)/shard_map/ppermute | solution.py:36
  285.3 26.4 %collective-permute-start.43 = (bf16[2,256,1024]{2,1,0:T(8,128)(2,1)}, bf16[2,256,1024]{2,1,0:T(8,128)(2,1)}, u32[]{:S(2)}, u32[]{:S(2)}) collective-permute-start(bf16[2,256,1024]{2,1,0:T(8,128)(2,1)} %grad_product.16), channel_id=1, source_target_pairs={{0,1},{1,0},{2,3},{3,2},{4,5},{5,4},{6,7},{7,6},{8,9},{9,8},{10,11... | collective-permute-start | bytes 3145736 | tf_op jit(solution)/shard_map/ppermute | solution.py:31
  298.2 44.0 %collective-permute-start.53 = (bf16[512,1024]{1,0:T(8,128)(2,1)}, bf16[512,1024]{1,0:T(8,128)(2,1)S(1)}, u32[]{:S(2)}, u32[]{:S(2)}) collective-permute-start(bf16[512,1024]{1,0:T(8,128)(2,1)} %return_product.4), channel_id=1, source_target_pairs={{0,1},{1,0},{2,3},{3,2},{4,5},{5,4},{6,7},{7,6},{8,9},{9,8},{10,11... | collective-permute-start | bytes 3145736 | tf_op jit(solution)/shard_map/ppermute | solution.py:31
  305.8 21.3 %collective-permute-start.44 = (bf16[512,768]{1,0:T(8,128)(2,1)S(1)}, bf16[512,768]{1,0:T(8,128)(2,1)S(1)}, u32[]{:S(2)}, u32[]{:S(2)}) collective-permute-start(bf16[512,768]{1,0:T(8,128)(2,1)S(1)} %fusion.29), channel_id=1, source_target_pairs={{4,6},{5,7},{2,0},{3,1},{12,14},{13,15},{10,8},{11,9},{20,22},{21,... | collective-permute-start | bytes 2359304 | tf_op jit(solution)/shard_map/ppermute | solution.py:36
  316.5 27.3 %collective-permute-start.45 = (bf16[2,256,768]{2,1,0:T(8,128)(2,1)S(1)}, bf16[2,256,768]{2,1,0:T(8,128)(2,1)S(1)}, u32[]{:S(2)}, u32[]{:S(2)}) collective-permute-start(bf16[2,256,768]{2,1,0:T(8,128)(2,1)S(1)} %get-tuple-element.156), channel_id=1, source_target_pairs={{0,8},{8,0},{16,24},{24,16},{1,9},{9,1},{17,25},{25,17},{2,10},{10... | collective-permute-start | bytes 2359304 | tf_op jit(solution)/shard_map/ppermute | solution.py:43
  316.6 28.9 %collective-permute-start.46 = (bf16[2,256,768]{2,1,0:T(8,128)(2,1)S(1)}, bf16[2,256,768]{2,1,0:T(8,128)(2,1)S(1)}, u32[]{:S(2)}, u32[]{:S(2)}) collective-permute-start(bf16[2,256,768]{2,1,0:T(8,128)(2,1)S(1)} %get-tuple-element.165), channel_id=1, source_target_pairs={{0,8},{8,0},{16,24},{24,16},{1,9},{9,1},{17,25},{25,17},{2,10},{10... | collective-permute-start | bytes 2359304 | tf_op jit(solution)/shard_map/ppermute | solution.py:43
  341.7 44.6 %collective-permute-start.59 = (bf16[512,1024]{1,0:T(8,128)(2,1)S(1)}, bf16[512,1024]{1,0:T(8,128)(2,1)}, u32[]{:S(2)}, u32[]{:S(2)}) collective-permute-start(bf16[512,1024]{1,0:T(8,128)(2,1)S(1)} %return_product.6), channel_id=1, source_target_pairs={{0,1},{1,0},{2,3},{3,2},{4,5},{5,4},{6,7},{7,6},{8,9},{9,8},{10,11... | collective-permute-start | bytes 3145736 | tf_op jit(solution)/shard_map/ppermute | solution.py:31
  342.2 43.9 %collective-permute-start.55 = (bf16[512,1024]{1,0:T(8,128)(2,1)S(1)}, bf16[512,1024]{1,0:T(8,128)(2,1)}, u32[]{:S(2)}, u32[]{:S(2)}) collective-permute-start(bf16[512,1024]{1,0:T(8,128)(2,1)S(1)} %collective-permute-done.53), channel_id=1, source_target_pairs={{0,16},{8,24},{16,0},{24,8},{1,17},{9,25},{17,1},{25,9},{2,18},{10... | collective-permute-start | bytes 3145736 | tf_op jit(solution)/shard_map/ppermute | solution.py:40
  345.5 45.2 %collective-permute-start.61 = (bf16[512,1024]{1,0:T(8,128)(2,1)S(1)}, bf16[512,1024]{1,0:T(8,128)(2,1)S(1)}, u32[]{:S(2)}, u32[]{:S(2)}) collective-permute-start(bf16[512,1024]{1,0:T(8,128)(2,1)S(1)} %return_product.7), channel_id=1, source_target_pairs={{0,16},{8,24},{16,0},{24,8},{1,17},{9,25},{17,1},{25,9},{2,18},{10... | collective-permute-start | bytes 3145736 | tf_op jit(solution)/shard_map/ppermute | solution.py:40
  347.7 36.8 %collective-permute-start.49 = (bf16[2,256,768]{2,1,0:T(8,128)(2,1)S(1)}, bf16[2,256,768]{2,1,0:T(8,128)(2,1)S(1)}, u32[]{:S(2)}, u32[]{:S(2)}) collective-permute-start(bf16[2,256,768]{2,1,0:T(8,128)(2,1)S(1)} %grad_product.20), channel_id=1, source_target_pairs={{0,1},{1,0},{2,3},{3,2},{4,5},{5,4},{6,7},{7,6},{8,9},{9,8},{10,11... | collective-permute-start | bytes 2359304 | tf_op jit(solution)/shard_map/ppermute | solution.py:31
  351.0 50.0 %collective-permute-start.50 = (bf16[2,256,768]{2,1,0:T(8,128)(2,1)S(1)}, bf16[2,256,768]{2,1,0:T(8,128)(2,1)S(1)}, u32[]{:S(2)}, u32[]{:S(2)}) collective-permute-start(bf16[2,256,768]{2,1,0:T(8,128)(2,1)S(1)} %grad_product.22), channel_id=1, source_target_pairs={{0,1},{1,0},{2,3},{3,2},{4,5},{5,4},{6,7},{7,6},{8,9},{9,8},{10,11... | collective-permute-start | bytes 2359304 | tf_op jit(solution)/shard_map/ppermute | solution.py:31
  386.2 48.5 %collective-permute-start.54 = (bf16[512,1024]{1,0:T(8,128)(2,1)S(1)}, bf16[512,1024]{1,0:T(8,128)(2,1)}, u32[]{:S(2)}, u32[]{:S(2)}) collective-permute-start(bf16[512,1024]{1,0:T(8,128)(2,1)S(1)} %collective-permute-done.53), channel_id=1, source_target_pairs={{0,8},{8,0},{16,24},{24,16},{1,9},{9,1},{17,25},{25,17},{2,10},{10... | collective-permute-start | bytes 3145736 | tf_op jit(solution)/shard_map/ppermute | solution.py:43
  386.3 48.4 %collective-permute-start.56 = (bf16[512,1024]{1,0:T(8,128)(2,1)}, bf16[512,1024]{1,0:T(8,128)(2,1)}, u32[]{:S(2)}, u32[]{:S(2)}) collective-permute-start(bf16[512,1024]{1,0:T(8,128)(2,1)} %collective-permute-done.55), channel_id=1, source_target_pairs={{0,8},{8,0},{16,24},{24,16},{1,9},{9,1},{17,25},{25,17},{2,10},{10... | collective-permute-start | bytes 3145736 | tf_op jit(solution)/shard_map/ppermute | solution.py:43
  390.7 50.6 %collective-permute-start.63 = (bf16[512,1024]{1,0:T(8,128)(2,1)}, bf16[512,1024]{1,0:T(8,128)(2,1)}, u32[]{:S(2)}, u32[]{:S(2)}) collective-permute-start(bf16[512,1024]{1,0:T(8,128)(2,1)} %collective-permute-done.59), channel_id=1, source_target_pairs={{0,16},{8,24},{16,0},{24,8},{1,17},{9,25},{17,1},{25,9},{2,18},{10... | collective-permute-start | bytes 3145736 | tf_op jit(solution)/shard_map/ppermute | solution.py:40
  401.0 47.1 %collective-permute-start.58 = (bf16[512,1024]{1,0:T(8,128)(2,1)S(1)}, bf16[512,1024]{1,0:T(8,128)(2,1)}, u32[]{:S(2)}, u32[]{:S(2)}) collective-permute-start(bf16[512,1024]{1,0:T(8,128)(2,1)S(1)} %return_product.7), channel_id=1, source_target_pairs={{0,8},{8,0},{16,24},{24,16},{1,9},{9,1},{17,25},{25,17},{2,10},{10... | collective-permute-start | bytes 3145736 | tf_op jit(solution)/shard_map/ppermute | solution.py:43
  401.9 30.1 %collective-permute-start.52 = (bf16[256,768]{1,0:T(8,128)(2,1)S(1)}, bf16[256,768]{1,0:T(8,128)(2,1)S(1)}, u32[]{:S(2)}, u32[]{:S(2)}) collective-permute-start(bf16[256,768]{1,0:T(8,128)(2,1)S(1)} %fusion.34), channel_id=1, source_target_pairs={{0,16},{8,24},{16,0},{24,8},{1,17},{9,25},{17,1},{25,9},{2,18},{10... | collective-permute-start | bytes 1179656 | tf_op jit(solution)/shard_map/ppermute | solution.py:40
  (82 other events, 929.1 us)
Sparse Core Ops, SparseCore 0:
  304.6 34.8 all-gather.3
